TPU v7x, 32 devices: a whole 2x2x4 slice. The times are simulated.
32 devices in a mesh: fsdp: 16 (over z, x, core), ctx: 2 (over y).
Axes of the slice: x: 2, y: 2, z: 4, core: 2. Of those that a mesh axis runs over, the one named last changes fastest.
Arguments:
- activations: bfloat16 [16, 1568, 1024], P('fsdp', 'ctx'), may hold values from -6 to 6
- cotangent: bfloat16 [16, 1568, 1024], P('fsdp', 'ctx'), may hold values from -6 to 6
- query_weight: bfloat16 [1024, 1024], P('fsdp'), may hold values from -0.1875 to 0.1875
- key_weight: bfloat16 [1024, 1024], P('fsdp'), may hold values from -0.1875 to 0.1875
- value_weight: bfloat16 [1024, 1024], P('fsdp'), may hold values from -0.1875 to 0.1875
- output_weight: bfloat16 [1024, 1024], P('fsdp'), may hold values from -1.5 to 1.5
- first_gain: bfloat16 [1024], P('fsdp'), may hold values from 0.25 to 1.75
- first_shift: bfloat16 [1024], P('fsdp'), may hold values from -2 to 2
- query_bias: bfloat16 [1024], P('fsdp'), may hold values from -2 to 2
- value_bias: bfloat16 [1024], P('fsdp'), may hold values from -2 to 2
- output_bias: bfloat16 [1024], P('fsdp'), may hold values from -2 to 2
- up_weight: bfloat16 [1024, 4096], P('fsdp'), may hold values from -0.1875 to 0.1875
- down_weight: bfloat16 [4096, 1024], P('fsdp'), may hold values from -0.09375 to 0.09375
- second_gain: bfloat16 [1024], P('fsdp'), may hold values from 0.25 to 1.75
- second_shift: bfloat16 [1024], P('fsdp'), may hold values from -2 to 2
- up_bias: bfloat16 [4096], P('fsdp'), may hold values from -2 to 2
- down_bias: bfloat16 [1024], P('fsdp'), may hold values from -2 to 2
Outputs:
- block_out: bfloat16 [16, 1568, 1024], P('fsdp', 'ctx')
- input_grad: float32 [16, 1568, 1024], P('fsdp', 'ctx')
- query_weight_grad: float32 [1024, 1024], P('fsdp')
- key_weight_grad: float32 [1024, 1024], P('fsdp')
- value_weight_grad: float32 [1024, 1024], P('fsdp')
- output_weight_grad: float32 [1024, 1024], P('fsdp')
- first_gain_grad: float32 [1024], P('fsdp')
- first_shift_grad: float32 [1024], P('fsdp')
- query_bias_grad: float32 [1024], P('fsdp')
- value_bias_grad: float32 [1024], P('fsdp')
- output_bias_grad: float32 [1024], P('fsdp')
- up_weight_grad: float32 [1024, 4096], P('fsdp')
- down_weight_grad: float32 [4096, 1024], P('fsdp')
- second_gain_grad: float32 [1024], P('fsdp')
- second_shift_grad: float32 [1024], P('fsdp')
- up_bias_grad: float32 [4096], P('fsdp')
- down_bias_grad: float32 [1024], P('fsdp')
All inputs are finite; a program needn't handle non-finite values.
Results may differ from a plain program's by a relative error of at most 0.02.
Values may be sent and summed in bfloat16 or wider, within the bound.
A program may use at most 384 MiB of HBM per device.

v0:
```python
import jax
import jax.numpy as jnp
from jax import lax
from jax.sharding import PartitionSpec as P

HEADS = 16
HDIM = 64


epsilon = 1e-05


def layer_norm(token_rows, gain, shift):
    centered = token_rows - jnp.mean(token_rows, axis=-1, keepdims=True)
    variance = jnp.mean(centered * centered, axis=-1, keepdims=True)
    return centered * lax.rsqrt(variance + epsilon) * gain + shift


def gelu_act(values_in):
    return jax.nn.gelu(values_in, approximate=True)


def gather_attention(shards):
    return (
        lax.all_gather(shards[0], "fsdp", axis=0, tiled=True),
        lax.all_gather(shards[1], "fsdp", axis=0, tiled=True),
        lax.all_gather(shards[2], "fsdp", axis=0, tiled=True),
        lax.all_gather(shards[3], "fsdp", axis=0, tiled=True),
        lax.all_gather(shards[4], "fsdp", axis=0, tiled=True),
        lax.all_gather(shards[5], "fsdp", axis=0, tiled=True),
        lax.all_gather(shards[6], "fsdp", axis=0, tiled=True),
        lax.all_gather(shards[7], "fsdp", axis=0, tiled=True),
        lax.all_gather(shards[8], "fsdp", axis=0, tiled=True),
    )


def gather_feed(shards):
    return (
        lax.all_gather(shards[0], "fsdp", axis=0, tiled=True),
        lax.all_gather(shards[1], "fsdp", axis=0, tiled=True),
        lax.all_gather(shards[2], "fsdp", axis=0, tiled=True),
        lax.all_gather(shards[3], "fsdp", axis=0, tiled=True),
        lax.all_gather(shards[4], "fsdp", axis=0, tiled=True),
        lax.all_gather(shards[5], "fsdp", axis=0, tiled=True),
    )


def on_device(
    activations,
    cotangent,
    query_weight,
    key_weight,
    value_weight,
    output_weight,
    first_gain,
    first_shift,
    query_bias,
    value_bias,
    output_bias,
    up_weight,
    down_weight,
    second_gain,
    second_shift,
    up_bias,
    down_bias,
):
    clip_count, local_len, width = activations.shape
    scaling = HDIM ** (-0.5)
    attend_shards = (
        query_weight,
        key_weight,
        value_weight,
        output_weight,
        first_gain,
        first_shift,
        query_bias,
        value_bias,
        output_bias,
    )
    feed_shards = (up_weight, down_weight, second_gain, second_shift, up_bias, down_bias)
    attend_full = gather_attention(attend_shards)
    (
        full_query,
        full_key,
        full_value,
        full_output,
        full_gain_one,
        full_shift_one,
        full_query_bias,
        full_value_bias,
        full_output_bias,
    ) = attend_full
    gain_one = full_gain_one.astype(jnp.float32)
    shift_one = full_shift_one.astype(jnp.float32)
    token_rows = activations.reshape(-1, width).astype(jnp.float32)
    normed_one = layer_norm(token_rows, gain_one, shift_one).astype(jnp.bfloat16)
    queries = (
        jnp.dot(normed_one, full_query, preferred_element_type=jnp.float32)
        + full_query_bias.astype(jnp.float32)
    ).astype(jnp.bfloat16)
    keys_local = jnp.dot(normed_one, full_key, preferred_element_type=jnp.float32).astype(
        jnp.bfloat16
    )
    values_local = (
        jnp.dot(normed_one, full_value, preferred_element_type=jnp.float32)
        + full_value_bias.astype(jnp.float32)
    ).astype(jnp.bfloat16)
    query_heads = queries.reshape(clip_count, local_len, HEADS, HDIM)
    keys_block = keys_local.reshape(clip_count, local_len, width)
    values_block = values_local.reshape(clip_count, local_len, width)
    run_max = jnp.full((clip_count, local_len, HEADS), -1e30, jnp.float32)
    key_piece = lax.all_gather(keys_block, "ctx", axis=1, tiled=True)
    value_piece = lax.all_gather(values_block, "ctx", axis=1, tiled=True)
    key_heads = key_piece.reshape(clip_count, -1, HEADS, HDIM)
    value_heads = value_piece.reshape(clip_count, -1, HEADS, HDIM)
    scores = (
        jnp.einsum("cqhd,ckhd->cqhk", query_heads, key_heads, preferred_element_type=jnp.float32)
        * scaling
    )
    new_max = jnp.maximum(run_max, jnp.max(scores, axis=-1))
    weights = jnp.exp(scores - new_max[..., None])
    run_sum = jnp.sum(weights, axis=-1)
    accum = jnp.einsum(
        "cqhk,ckhd->cqhd",
        weights.astype(jnp.bfloat16),
        value_heads,
        preferred_element_type=jnp.float32,
    )
    run_max, run_sum, accum = (new_max, run_sum, accum)
    attend_exact = accum / run_sum[..., None]
    log_total = run_max + jnp.log(run_sum)
    attended = attend_exact.reshape(-1, width).astype(jnp.bfloat16)
    mid_rows = (
        token_rows
        + jnp.dot(attended, full_output, preferred_element_type=jnp.float32)
        + full_output_bias.astype(jnp.float32)
    )
    feed_full = gather_feed(feed_shards)
    full_up, full_down, full_gain_two, full_shift_two, full_up_bias, full_down_bias = feed_full
    gain_two = full_gain_two.astype(jnp.float32)
    shift_two = full_shift_two.astype(jnp.float32)
    normed_two = layer_norm(mid_rows, gain_two, shift_two).astype(jnp.bfloat16)
    pre_act = jnp.dot(
        normed_two, full_up, preferred_element_type=jnp.float32
    ) + full_up_bias.astype(jnp.float32)
    hidden = gelu_act(pre_act).astype(jnp.bfloat16)
    block_rows = (
        mid_rows
        + jnp.dot(hidden, full_down, preferred_element_type=jnp.float32)
        + full_down_bias.astype(jnp.float32)
    )
    block_out = block_rows.astype(jnp.bfloat16).reshape(activations.shape)
    back_attend = gather_attention(attend_shards)
    back_feed = gather_feed(feed_shards)
    back_query, back_key, back_value, back_output = (
        back_attend[0],
        back_attend[1],
        back_attend[2],
        back_attend[3],
    )
    back_up, back_down = (back_feed[0], back_feed[1])
    cot_rows = cotangent.reshape(-1, width)
    outer_grad = cot_rows.astype(jnp.float32)
    down_wgrad = jnp.einsum("rf,rd->fd", hidden, cot_rows, preferred_element_type=jnp.float32)
    down_bgrad = jnp.sum(outer_grad, axis=0)
    hidden_grad = jnp.einsum("rd,fd->rf", cot_rows, back_down, preferred_element_type=jnp.float32)
    _, gelu_back = jax.vjp(gelu_act, pre_act)
    pre_grad = gelu_back(hidden_grad)[0].astype(jnp.bfloat16)
    up_wgrad = jnp.einsum("rd,rf->df", normed_two, pre_grad, preferred_element_type=jnp.float32)
    up_bgrad = jnp.sum(pre_grad.astype(jnp.float32), axis=0)
    normed_two_grad = jnp.einsum("rf,df->rd", pre_grad, back_up, preferred_element_type=jnp.float32)
    _, norm_two_back = jax.vjp(layer_norm, mid_rows, gain_two, shift_two)
    mid_part, gain_two_grad, shift_two_grad = norm_two_back(normed_two_grad)
    mid_grad = outer_grad + mid_part
    feed_owned = (
        lax.psum_scatter(
            up_wgrad.astype(jnp.bfloat16), "fsdp", scatter_dimension=0, tiled=True
        ).astype(jnp.float32),
        lax.psum_scatter(
            down_wgrad.astype(jnp.bfloat16), "fsdp", scatter_dimension=0, tiled=True
        ).astype(jnp.float32),
        lax.psum_scatter(
            gain_two_grad.astype(jnp.bfloat16), "fsdp", scatter_dimension=0, tiled=True
        ).astype(jnp.float32),
        lax.psum_scatter(
            shift_two_grad.astype(jnp.bfloat16), "fsdp", scatter_dimension=0, tiled=True
        ).astype(jnp.float32),
        lax.psum_scatter(
            up_bgrad.astype(jnp.bfloat16), "fsdp", scatter_dimension=0, tiled=True
        ).astype(jnp.float32),
        lax.psum_scatter(
            down_bgrad.astype(jnp.bfloat16), "fsdp", scatter_dimension=0, tiled=True
        ).astype(jnp.float32),
    )
    feed_done = (
        lax.psum(feed_owned[0].astype(jnp.bfloat16), "ctx").astype(jnp.float32),
        lax.psum(feed_owned[1].astype(jnp.bfloat16), "ctx").astype(jnp.float32),
        lax.psum(feed_owned[2].astype(jnp.bfloat16), "ctx").astype(jnp.float32),
        lax.psum(feed_owned[3].astype(jnp.bfloat16), "ctx").astype(jnp.float32),
        lax.psum(feed_owned[4].astype(jnp.bfloat16), "ctx").astype(jnp.float32),
        lax.psum(feed_owned[5].astype(jnp.bfloat16), "ctx").astype(jnp.float32),
    )
    branch_grad = mid_grad.astype(jnp.bfloat16)
    output_wgrad = jnp.einsum(
        "rd,re->de", attended, branch_grad, preferred_element_type=jnp.float32
    )
    output_bgrad = jnp.sum(branch_grad.astype(jnp.float32), axis=0)
    attended_grad = jnp.einsum(
        "re,de->rd", branch_grad, back_output, preferred_element_type=jnp.float32
    ).astype(jnp.bfloat16)
    grad_heads = attended_grad.reshape(clip_count, local_len, HEADS, HDIM)
    delta = jnp.sum(grad_heads.astype(jnp.float32) * attend_exact, axis=-1)
    keys_whole, values_whole = (
        lax.all_gather(keys_block, "ctx", axis=1, tiled=True),
        lax.all_gather(values_block, "ctx", axis=1, tiled=True),
    )
    key_heads_all = keys_whole.reshape(clip_count, -1, HEADS, HDIM)
    value_heads_all = values_whole.reshape(clip_count, -1, HEADS, HDIM)
    scores_all = (
        jnp.einsum(
            "cqhd,ckhd->cqhk", query_heads, key_heads_all, preferred_element_type=jnp.float32
        )
        * scaling
    )
    probs = jnp.exp(scores_all - log_total[..., None])
    prob_grad = jnp.einsum(
        "cqhd,ckhd->cqhk", grad_heads, value_heads_all, preferred_element_type=jnp.float32
    )
    score_grad = (probs * (prob_grad - delta[..., None])).astype(jnp.bfloat16)
    query_grad = (
        jnp.einsum("cqhk,ckhd->cqhd", score_grad, key_heads_all, preferred_element_type=jnp.float32)
        * scaling
    ).astype(jnp.bfloat16)
    query_grad = query_grad.reshape(-1, width)
    probs_low = probs.astype(jnp.bfloat16)
    key_part = (
        jnp.einsum("cqhk,cqhd->kchd", score_grad, query_heads, preferred_element_type=jnp.float32)
        * scaling
    )
    value_part = jnp.einsum(
        "cqhk,cqhd->kchd", probs_low, grad_heads, preferred_element_type=jnp.float32
    )
    summed = lax.psum_scatter(
        jnp.stack([key_part, value_part], axis=2)
        .reshape(lax.axis_size("ctx") * local_len, clip_count, 2, width)
        .astype(jnp.bfloat16),
        "ctx",
        scatter_dimension=0,
        tiled=True,
    ).astype(jnp.float32)
    key_grad = jnp.transpose(summed[:, :, 0], (1, 0, 2)).reshape(-1, width).astype(jnp.bfloat16)
    value_grad = jnp.transpose(summed[:, :, 1], (1, 0, 2)).reshape(-1, width).astype(jnp.bfloat16)
    query_wgrad = jnp.einsum(
        "rd,re->de", normed_one, query_grad, preferred_element_type=jnp.float32
    )
    key_wgrad = jnp.einsum("rd,re->de", normed_one, key_grad, preferred_element_type=jnp.float32)
    value_wgrad = jnp.einsum(
        "rd,re->de", normed_one, value_grad, preferred_element_type=jnp.float32
    )
    query_bgrad = jnp.sum(query_grad.astype(jnp.float32), axis=0)
    value_bgrad = jnp.sum(value_grad.astype(jnp.float32), axis=0)
    normed_one_grad = (
        jnp.einsum("re,de->rd", query_grad, back_query, preferred_element_type=jnp.float32)
        + jnp.einsum("re,de->rd", key_grad, back_key, preferred_element_type=jnp.float32)
        + jnp.einsum("re,de->rd", value_grad, back_value, preferred_element_type=jnp.float32)
    )
    _, norm_one_back = jax.vjp(layer_norm, token_rows, gain_one, shift_one)
    input_part, gain_one_grad, shift_one_grad = norm_one_back(normed_one_grad)
    input_grad = (mid_grad + input_part).reshape(activations.shape)
    attend_owned = (
        lax.psum_scatter(
            query_wgrad.astype(jnp.bfloat16), "fsdp", scatter_dimension=0, tiled=True
        ).astype(jnp.float32),
        lax.psum_scatter(
            key_wgrad.astype(jnp.bfloat16), "fsdp", scatter_dimension=0, tiled=True
        ).astype(jnp.float32),
        lax.psum_scatter(
            value_wgrad.astype(jnp.bfloat16), "fsdp", scatter_dimension=0, tiled=True
        ).astype(jnp.float32),
        lax.psum_scatter(
            output_wgrad.astype(jnp.bfloat16), "fsdp", scatter_dimension=0, tiled=True
        ).astype(jnp.float32),
        lax.psum_scatter(
            gain_one_grad.astype(jnp.bfloat16), "fsdp", scatter_dimension=0, tiled=True
        ).astype(jnp.float32),
        lax.psum_scatter(
            shift_one_grad.astype(jnp.bfloat16), "fsdp", scatter_dimension=0, tiled=True
        ).astype(jnp.float32),
        lax.psum_scatter(
            query_bgrad.astype(jnp.bfloat16), "fsdp", scatter_dimension=0, tiled=True
        ).astype(jnp.float32),
        lax.psum_scatter(
            value_bgrad.astype(jnp.bfloat16), "fsdp", scatter_dimension=0, tiled=True
        ).astype(jnp.float32),
        lax.psum_scatter(
            output_bgrad.astype(jnp.bfloat16), "fsdp", scatter_dimension=0, tiled=True
        ).astype(jnp.float32),
    )
    attend_done = (
        lax.psum(attend_owned[0].astype(jnp.bfloat16), "ctx").astype(jnp.float32),
        lax.psum(attend_owned[1].astype(jnp.bfloat16), "ctx").astype(jnp.float32),
        lax.psum(attend_owned[2].astype(jnp.bfloat16), "ctx").astype(jnp.float32),
        lax.psum(attend_owned[3].astype(jnp.bfloat16), "ctx").astype(jnp.float32),
        lax.psum(attend_owned[4].astype(jnp.bfloat16), "ctx").astype(jnp.float32),
        lax.psum(attend_owned[5].astype(jnp.bfloat16), "ctx").astype(jnp.float32),
        lax.psum(attend_owned[6].astype(jnp.bfloat16), "ctx").astype(jnp.float32),
        lax.psum(attend_owned[7].astype(jnp.bfloat16), "ctx").astype(jnp.float32),
        lax.psum(attend_owned[8].astype(jnp.bfloat16), "ctx").astype(jnp.float32),
    )
    return (
        block_out,
        input_grad,
        attend_done[0],
        attend_done[1],
        attend_done[2],
        attend_done[3],
        attend_done[4],
        attend_done[5],
        attend_done[6],
        attend_done[7],
        attend_done[8],
        feed_done[0],
        feed_done[1],
        feed_done[2],
        feed_done[3],
        feed_done[4],
        feed_done[5],
    )


def solution(mesh):
    return jax.shard_map(
        on_device,
        mesh=mesh,
        in_specs=(
            P("fsdp", "ctx", None),
            P("fsdp", "ctx", None),
            P("fsdp", None),
            P("fsdp", None),
            P("fsdp", None),
            P("fsdp", None),
            P("fsdp"),
            P("fsdp"),
            P("fsdp"),
            P("fsdp"),
            P("fsdp"),
            P("fsdp", None),
            P("fsdp", None),
            P("fsdp"),
            P("fsdp"),
            P("fsdp"),
            P("fsdp"),
        ),
        out_specs=(
            P("fsdp", "ctx", None),
            P("fsdp", "ctx", None),
            P("fsdp", None),
            P("fsdp", None),
            P("fsdp", None),
            P("fsdp", None),
            P("fsdp"),
            P("fsdp"),
            P("fsdp"),
            P("fsdp"),
            P("fsdp"),
            P("fsdp", None),
            P("fsdp", None),
            P("fsdp"),
            P("fsdp"),
            P("fsdp"),
            P("fsdp"),
        ),
        check_vma=False,
    )
```

profile of v0, /device:TPU:0, one launch (start us, length us, event | category | flops | bytes accessed | tf_op | source)
XLA Modules:
  0.0 1320.8 jit_solution(9385595821402023116)
XLA Ops:
  17.3 63.2 %all-reduce.19 = (bf16[1024]{0:T(1024)(128)(2,1)S(1)}, bf16[1024]{0:T(1024)(128)(2,1)S(1)}, bf16[1024]{0:T(1024)(128)(2,1)S(1)}, bf16[1024]{0:T(1024)(128)(2,1)S...) all-reduce(bf16[1024]{0:T(1024)(128)(2,1)S(1)} %dynamic-update-slic, ...), channel_id=1, replica_groups=mesh['fsdp'=16,'ctx'=2] {'fsdp'}, use_global_device_ids=true, to_apply=%add.2 | all-reduce | flops 7168 | bytes 28672
  87.7 9.2 all-gather.14.cloned.1.call-done
  104.3 19.2 %all-gather.2 = bf16[16,1,256]{2,1,0:T(2,128)(2,1)S(1)} all-gather(bf16[1,1,256]{2,1,0:T(2,128)(2,1)S(1)} %reshape.388), channel_id=1, replica_groups=mesh['fsdp'=16,'ctx'=2] {'fsdp'}, dimensions={0}, use_global_device_ids=true | all-gather | bytes 8704 | tf_op jit(solution)/shard_map/all_gather | solution.py:43
  123.5 15.8 %all-gather.16.cloned.1.call-done = bf16[1024,1024]{1,0:T(8,128)(2,1)} async-done(((bf16[64,1024]{1,0:T(8,128)(2,1)}), bf16[1024,1024]{1,0:T(8,128)(2,1)}) %all-gather.16.cloned.1.call-update) | async-done | bytes 2097168 | tf_op jit(solution)/shard_map/all_gather | solution.py:25
  145.8 39.9 %all-gather.24.cloned.1.call-done = bf16[1568,1024]{1,0:T(8,128)(2,1)} async-done(((bf16[784,1024]{1,0:T(8,128)(2,1)}), bf16[1568,1024]{1,0:T(8,128)(2,1)}) %all-gather.24.cloned.1.call-update) | async-done | bytes 3211280 | tf_op jit(solution)/shard_map/all_gather | solution.py:113
  191.0 42.3 %all-gather.26.cloned.1.call-done = bf16[1568,1024]{1,0:T(8,128)(2,1)} async-done(((bf16[784,1024]{1,0:T(8,128)(2,1)}), bf16[1568,1024]{1,0:T(8,128)(2,1)}) %all-gather.26.cloned.1.call-update) | async-done | bytes 3211280 | tf_op jit(solution)/shard_map/all_gather | solution.py:112
  237.7 31.7 %bitcast_reduce_fusion = (f32[784,16]{0,1:T(8,128)S(1)}, f32[16,1568,784]{1,2,0:T(8,128)}) fusion(bf16[1568,16,64]{0,2,1:T(8,128)(2,1)S(1)} %bitcast.188, bf16[784,16,64]{0,2,1:T(8,128)(2,1)} %bitcast.192), kind=kOutput, calls=%fused_computation.5 | convolution fusion | flops 2556956416 | bytes 83543040 | tf_op jit(solution)/shard_map/cqhd,ckhd->cqhk/dot_general | solution.py:117
  270.0 27.0 %fusion.5 = f32[784,16]{0,1:T(8,128)S(1)} fusion(f32[16,1568,784]{1,2,0:T(8,128)} %get-tuple-element.65, f32[784,16]{0,1:T(8,128)S(1)} %broadcast_maximum_fusion), kind=kLoop, calls=%fused_computation.9 | loop fusion | flops 58994432 | bytes 78776320 | tf_op jit(solution)/shard_map/reduce_sum | solution.py:122
  297.0 32.8 %fusion.83 = (bf16[1,784,16,64]{1,3,2,0:T(8,128)(2,1)}, f32[1,784,16,64]{1,3,2,0:T(8,128)}) fusion(f32[784,16]{0,1:T(8,128)S(1)} %fusion.5, bf16[1568,16,64]{0,2,1:T(8,128)(2,1)S(1)} %bitcast.190, f32[16,1568,784]{1,2,0:T(8,128)} %get-tuple-element.65, f32[784,16]{0,1:T(8,128)S(1)} %broadcast_maximum_fusion), kind=kOutput, calls=%fused_computation.113 | convolution fusion | flops 2578243584 | bytes 86804480 | tf_op jit(solution)/shard_map/cqhk,ckhd->cqhd/dot_general | solution.py:123
  336.9 15.8 %all-gather.20.cloned.1.call-done = bf16[1024,4096]{1,0:T(8,128)(2,1)} async-done(((bf16[64,4096]{1,0:T(8,128)(2,1)}), bf16[1024,4096]{1,0:T(8,128)(2,1)}) %all-gather.20.cloned.1.call-update) | async-done | bytes 8388624 | tf_op jit(solution)/shard_map/all_gather | solution.py:39
  352.7 13.2 %fusion.69 = f32[784,4096]{1,0:T(8,128)} fusion(bf16[1024,4096]{1,0:T(8,128)(2,1)} %all-gather.20.cloned.1.call-done, f32[784,1024]{1,0:T(8,128)} %copy-done.10, f32[1024]{0:T(1024)} %convert_element_type.269, f32[1024]{0:T(1024)S(1)} %convert_element_type.268, f32[784]{0:T(1024)S(1)} %fusion.64, f32[784]{0:T(1024)S(1)} %broadcast_multiply_fusion), kind=kOutput, calls=%fused_computation.107 | convolution fusion | flops 6580682752 | bytes 24459392 | tf_op jit(solution)/shard_map/dot_general | solution.py:143
  365.9 62.1 %all-gather.22.cloned.1.call-done = bf16[4096,1024]{1,0:T(8,128)(2,1)} async-done(((bf16[256,1024]{1,0:T(8,128)(2,1)}), bf16[4096,1024]{1,0:T(8,128)(2,1)}) %all-gather.22.cloned.1.call-update) | async-done | bytes 8388624 | tf_op jit(solution)/shard_map/all_gather | solution.py:40
  428.1 21.2 %fusion.77 = (bf16[4096]{0:T(1024)(128)(2,1)}, bf16[784,4096]{1,0:T(8,128)(2,1)}) fusion(f32[784,4096]{1,0:T(8,128)} %fusion.69, f32[4096]{0:T(1024)S(1)} %bitcast.203, bf16[4096,1024]{1,0:T(8,128)(2,1)} %all-gather.22.cloned.1.call-done, bf16[1,784,1024]{2,1,0:T(8,128)(2,1)} %param.18), kind=kOutput, calls=%fused_computation.109 | convolution fusion | flops 6647312384 | bytes 29286400 | tf_op jit(solution)/shard_map/rd,fd->rf/dot_general | solution.py:166
  449.3 12.8 multiply_reduce_fusion.1
  480.5 31.0 %fusion.32 = bf16[16,64,1568]{2,1,0:T(8,128)(2,1)} fusion(bf16[784,16,64]{0,2,1:T(8,128)(2,1)} %bitcast.194, f32[16,1568,784]{1,2,0:T(8,128)} %get-tuple-element.65, f32[784,16]{0,1:T(8,128)S(1)} %log_add_fusion), kind=kOutput, calls=%fused_computation.44 | convolution fusion | flops 2578243584 | bytes 83543040 | tf_op jit(solution)/shard_map/cqhk,cqhd->kchd/dot_general | solution.py:240
  511.5 44.0 %fusion.1 = bf16[1,784,16,1568]{3,1,2,0:T(8,128)(2,1)} fusion(f32[16,1568,784]{1,2,0:T(8,128)} %get-tuple-element.65, bf16[1568,16,64]{0,2,1:T(8,128)(2,1)S(1)} %bitcast.191, bf16[784,16,64]{0,2,1:T(8,128)(2,1)} %bitcast.195, f32[784,16]{0,1:T(8,128)S(1)} %multiply_reduce_fusion, f32[784,16]{0,1:T(8,128)S(1)} %log_add_fusion), kind=kOutput, calls=%fused_computation.2 | convolution fusion | flops 2615975936 | bytes 122931200 | tf_op jit(solution)/shard_map/cqhd,ckhd->cqhk/dot_general | solution.py:226
  555.5 18.7 %multiply_convert_fusion.1 = bf16[16,64,1568]{2,1,0:T(8,128)(2,1)} fusion(bf16[784,16,64]{0,2,1:T(8,128)(2,1)} %bitcast.193, bf16[1,784,16,1568]{3,1,2,0:T(8,128)(2,1)} %fusion.1), kind=kOutput, calls=%fused_computation.31 | convolution fusion | flops 2520842240 | bytes 44154880 | tf_op jit(solution)/shard_map/cqhk,cqhd->kchd/dot_general | solution.py:237
  574.2 12.1 copy.61
  586.3 16.4 %copy.60 = bf16[1568,1,1,1024]{3,2,1,0:T(2,128)(2,1)} copy(bf16[1568,1,1,1024]{0,3,2,1:T(8,128)(2,1)} %bitcast.197) | data formatting | bytes 6422528 | tf_op jit(solution)/shard_map/stack | solution.py:244
  602.7 15.8 %pad_maximum_fusion = bf16[1568,1,2,1024]{3,2,1,0:T(2,128)(2,1)} fusion(bf16[1568,1,1,1024]{3,2,1,0:T(2,128)(2,1)} %copy.61, bf16[1568,1,1,1024]{3,2,1,0:T(2,128)(2,1)} %copy.60), kind=kLoop, calls=%fused_computation.32 | loop fusion | flops 12845056 | bytes 12845056 | tf_op jit(solution)/shard_map/stack | solution.py:244
  624.5 21.1 %bitcast_reduce_fusion.1 = (bf16[16,64]{1,0:T(8,128)(2,1)S(1)}, bf16[16,64,784]{2,1,0:T(8,128)(2,1)}) fusion(bf16[1568,16,64]{0,2,1:T(8,128)(2,1)S(1)} %bitcast.189, bf16[1,784,16,1568]{3,1,2,0:T(8,128)(2,1)} %fusion.1), kind=kOutput, calls=%fused_computation.78 | convolution fusion | flops 2520038400 | bytes 44156928 | tf_op jit(solution)/shard_map/cqhk,ckhd->cqhd/dot_general | solution.py:231
  645.6 6.1 convolution_convert_fusion.3
  653.0 120.0 %all-reduce.25.cloned.1.call-done = bf16[1568,1,2,1024]{3,2,1,0:T(2,128)(2,1)} async-done(((bf16[1568,1,2,1024]{3,2,1,0:T(2,128)(2,1)}), bf16[1568,1,2,1024]{3,2,1,0:T(2,128)(2,1)}) %all-reduce.25.cloned.1.call-update) | async-done | bytes 6422544
  789.7 14.8 %convolution_convert_fusion = bf16[1024,4096]{1,0:T(8,128)(2,1)} fusion(bf16[784,4096]{1,0:T(8,128)(2,1)} %get-tuple-element.57, f32[784,1024]{1,0:T(8,128)} %copy-done.10, f32[1024]{0:T(1024)S(1)} %copy-done.41, f32[1024]{0:T(1024)S(1)} %copy-done.32, f32[784]{0:T(1024)S(1)} %copy-done.34, f32[784]{0:T(1024)S(1)} %copy-done.28), kind=kOutput, calls=%fused_computation.29 | convolution fusion | flops 6584877056 | bytes 18036864 | tf_op jit(solution)/shard_map/rd,rf->df/dot_general | solution.py:169
  805.9 16.7 %convolution_convert_fusion.1 = bf16[4096,1024]{1,0:T(8,128)(2,1)} fusion(bf16[1,784,1024]{2,1,0:T(8,128)(2,1)S(1)} %copy-done.9, f32[784,4096]{1,0:T(8,128)} %fusion.69, f32[4096]{0:T(1024)S(1)} %bitcast.204), kind=kOutput, calls=%fused_computation.30 | convolution fusion | flops 6612975616 | bytes 22855680 | tf_op jit(solution)/shard_map/rf,rd->fd/dot_general | solution.py:164
  835.8 62.4 %all-reduce.18 = (bf16[1024]{0:T(1024)(128)(2,1)S(1)}, bf16[1024]{0:T(1024)(128)(2,1)S(1)}, bf16[1024]{0:T(1024)(128)(2,1)S(1)}, bf16[1024]{0:T(1024)(128)(2,1)S...) all-reduce(bf16[1024]{0:T(1024)(128)(2,1)S(1)} %dynamic-update-slic, ...), channel_id=1, replica_groups=mesh['fsdp'=16,'ctx'=2] {'fsdp'}, use_global_device_ids=true, to_apply=%add.7 | all-reduce | flops 13312 | bytes 53248
  903.3 64.7 %reduce-scatter.9.cloned.1.call-done = bf16[64,1024]{1,0:T(8,128)(2,1)} async-done(((bf16[1024,1024]{1,0:T(8,128)(2,1)}), bf16[64,1024]{1,0:T(8,128)(2,1)}) %reduce-scatter.9.cloned.1.call-update) | async-done | bytes 131088 | tf_op jit(solution)/shard_map/reduce_scatter | solution.py:274
  968.0 64.2 %reduce-scatter.11.cloned.1.call-done = bf16[64,1024]{1,0:T(8,128)(2,1)} async-done(((bf16[1024,1024]{1,0:T(8,128)(2,1)}), bf16[64,1024]{1,0:T(8,128)(2,1)}) %reduce-scatter.11.cloned.1.call-update) | async-done | bytes 131088 | tf_op jit(solution)/shard_map/reduce_scatter | solution.py:277
  1032.2 108.1 %reduce-scatter.15.cloned.1.call-done = bf16[64,4096]{1,0:T(8,128)(2,1)} async-done(((bf16[1024,4096]{1,0:T(8,128)(2,1)}), bf16[64,4096]{1,0:T(8,128)(2,1)}) %reduce-scatter.15.cloned.1.call-update) | async-done | bytes 524304 | tf_op jit(solution)/shard_map/reduce_scatter | solution.py:176
  1140.4 108.9 %reduce-scatter.17.cloned.1.call-done = bf16[256,1024]{1,0:T(8,128)(2,1)} async-done(((bf16[4096,1024]{1,0:T(8,128)(2,1)}), bf16[256,1024]{1,0:T(8,128)(2,1)}) %reduce-scatter.17.cloned.1.call-update) | async-done | bytes 524304 | tf_op jit(solution)/shard_map/reduce_scatter | solution.py:179
  1249.3 15.3 %fusion.52 = bf16[1,784,1024]{2,1,0:T(8,128)(2,1)} fusion(f32[784,1024]{1,0:T(8,128)} %copy-done.10, f32[1024]{0:T(1024)S(1)} %convert_element_type.273, bf16[4096,1024]{1,0:T(8,128)(2,1)} %all-gather.22.cloned.1.call-done, f32[784,4096]{1,0:T(8,128)} %fusion.69, f32[4096]{0:T(1024)S(1)} %bitcast.205), kind=kOutput, calls=%fused_computation.81 | convolution fusion | flops 6611189760 | bytes 26071040 | tf_op jit(solution)/shard_map/dot_general | solution.py:149
  1279.9 24.5 %all-reduce.27.cloned.1.call-done = (bf16[64,1024]{1,0:T(8,128)(2,1)}, bf16[64,1024]{1,0:T(8,128)(2,1)}, bf16[64,1024]{1,0:T(8,128)(2,1)}, bf16[64,1024]{1,0:T(8...) async-done(((bf16[64,1024]{1,0:T(8,128)(2,1)}, bf16[64,1024]{1,0:T(8,128)(2,1)}, bf16[64,1024]{1,0:T(8,128)(2,1)}, bf16[64,1024]{1,0:T(8,128)(2,1)}, ...) | async-done | bytes 1572880 | tf_op jit(solution)/shard_map/psum | solution.py:300
  (228 shorter events, 132.4 us)
Async XLA Ops:
  7.2 75.1 %copy-start.5 = (bf16[1,784,1024]{2,1,0:T(8,128)(2,1)S(1)}, bf16[1,784,1024]{2,1,0:T(8,128)(2,1)}, u32[]{:S(2)}) copy-start(bf16[1,784,1024]{2,1,0:T(8,128)(2,1)} %param.17) | copy-start | bytes 4816900
  7.2 75.8 %all-gather.12.cloned.1.call-start = ((), (), s32[]{:S(2)}) async-start(), calls=%async_computation.6 | async-start | bytes 2228224 | tf_op jit(solution)/shard_map/all_gather | solution.py:27
  7.9 88.9 %all-gather.14.cloned.1.call-start = ((), (), s32[]{:S(2)}) async-start(), calls=%async_computation.7 | async-start | bytes 2228224 | tf_op jit(solution)/shard_map/all_gather | solution.py:26
  8.7 130.6 %all-gather.16.cloned.1.call-start = ((), (), s32[]{:S(2)}) async-start(), calls=%async_computation.8 | async-start | bytes 2228224 | tf_op jit(solution)/shard_map/all_gather | solution.py:25
  9.4 176.3 %all-gather.24.cloned.1.call-start = ((), (), s32[]{:S(2)}) async-start(), calls=%async_computation.18 | async-start | bytes 4816896 | tf_op jit(solution)/shard_map/all_gather | solution.py:113
  80.6 58.7 %copy-start.21 = (f32[1024]{0:T(1024)}, f32[1024]{0:T(1024)S(1)}, u32[]{:S(2)}) copy-start(f32[1024]{0:T(1024)S(1)} %convert_element_type.256) | copy-start | bytes 12292
  80.6 58.7 %copy-start.39 = (f32[1024]{0:T(1024)}, f32[1024]{0:T(1024)S(1)}, u32[]{:S(2)}) copy-start(f32[1024]{0:T(1024)S(1)} %convert_element_type.257) | copy-start | bytes 12292
  82.3 56.9 %copy-start.19 = (f32[784]{0:T(1024)}, f32[784]{0:T(1024)S(1)}, u32[]{:S(2)}) copy-start(f32[784]{0:T(1024)S(1)} %broadcast_multiply_fusion.1) | copy-start | bytes 9412
  82.9 56.3 %copy-start.23 = (f32[784]{0:T(1024)}, f32[784]{0:T(1024)S(1)}, u32[]{:S(2)}) copy-start(f32[784]{0:T(1024)S(1)} %fusion.63) | copy-start | bytes 9412
  87.7 145.7 %all-gather.26.cloned.1.call-start = ((), (), s32[]{:S(2)}) async-start(), calls=%async_computation.19 | async-start | bytes 4816896 | tf_op jit(solution)/shard_map/all_gather | solution.py:112
  101.5 228.3 %all-gather.18.cloned.1.call-start = ((), (), s32[]{:S(2)}) async-start(), calls=%async_computation.9 | async-start | bytes 2228224 | tf_op jit(solution)/shard_map/all_gather | solution.py:28
  102.1 250.6 %all-gather.20.cloned.1.call-start = ((), (), s32[]{:S(2)}) async-start(), calls=%async_computation.10 | async-start | bytes 8912896 | tf_op jit(solution)/shard_map/all_gather | solution.py:39
  102.9 325.2 %all-gather.22.cloned.1.call-start = ((), (), s32[]{:S(2)}) async-start(), calls=%async_computation.11 | async-start | bytes 8912896 | tf_op jit(solution)/shard_map/all_gather | solution.py:40
  103.6 669.4 %all-reduce.25.cloned.1.call-start = ((), (), s32[]{:S(2)}) async-start(), calls=%async_computation.20 | async-start | bytes 12845056
  103.7 358.4 %copy-start.31 = (f32[1024]{0:T(1024)}, f32[1024]{0:T(1024)S(1)}, u32[]{:S(2)}) copy-start(f32[1024]{0:T(1024)S(1)} %convert_element_type.268) | copy-start | bytes 12292
  123.5 304.6 %copy-start.35 = (f32[16,1,256]{2,1,0:T(1,128)}, f32[16,1,256]{2,1,0:T(1,128)S(1)}, u32[]{:S(2)}) copy-start(f32[16,1,256]{2,1,0:T(1,128)S(1)} %convert_element_type.319) | copy-start | bytes 49156
  237.7 31.7 %copy-start = (bf16[1568,1024]{0,1:T(8,128)(2,1)}, bf16[1568,1024]{0,1:T(8,128)(2,1)S(1)}, u32[]{:S(2)}) copy-start(bf16[1568,1024]{0,1:T(8,128)(2,1)S(1)} %copy.56) | copy-start | bytes 9633796
  270.0 27.0 %copy-start.2 = (bf16[1568,1024]{0,1:T(8,128)(2,1)S(1)}, bf16[1568,1024]{0,1:T(8,128)(2,1)}, u32[]{:S(2)}) copy-start(bf16[1568,1024]{0,1:T(8,128)(2,1)} %copy.55) | copy-start | bytes 9633796
  334.7 127.4 %copy-start.27 = (f32[784]{0:T(1024)}, f32[784]{0:T(1024)S(1)}, u32[]{:S(2)}) copy-start(f32[784]{0:T(1024)S(1)} %broadcast_multiply_fusion) | copy-start | bytes 9412
  336.9 125.2 %copy-start.33 = (f32[784]{0:T(1024)}, f32[784]{0:T(1024)S(1)}, u32[]{:S(2)}) copy-start(f32[784]{0:T(1024)S(1)} %fusion.64) | copy-start | bytes 9412
  428.1 21.2 %copy-start.11 = (f32[784,1024]{1,0:T(8,128)S(1)}, f32[784,1024]{1,0:T(8,128)}, u32[]{:S(2)}) copy-start(f32[784,1024]{1,0:T(8,128)} %copy-done.10) | copy-start | bytes 9633796
  618.5 279.7 %reduce-scatter.13.cloned.1.call-start = ((), (), s32[]{:S(2)}) async-start(), calls=%async_computation.15 | async-start | bytes 2228224 | tf_op jit(solution)/shard_map/reduce_scatter | solution.py:280
  624.4 21.2 %copy-start.20 = (f32[784]{0:T(1024)S(1)}, f32[784]{0:T(1024)}, u32[]{:S(2)}) copy-start(f32[784]{0:T(1024)} %copy-done.19) | copy-start | bytes 9412
  624.4 21.2 %copy-start.22 = (f32[1024]{0:T(1024)S(1)}, f32[1024]{0:T(1024)}, u32[]{:S(2)}) copy-start(f32[1024]{0:T(1024)} %copy-done.21) | copy-start | bytes 12292
  624.4 278.9 %reduce-scatter.7.cloned.1.call-start = ((), (), s32[]{:S(2)}) async-start(), calls=%async_computation.12 | async-start | bytes 2228224 | tf_op jit(solution)/shard_map/reduce_scatter | solution.py:271
  651.7 316.3 %reduce-scatter.9.cloned.1.call-start = ((), (), s32[]{:S(2)}) async-start(), calls=%async_computation.13 | async-start | bytes 2228224 | tf_op jit(solution)/shard_map/reduce_scatter | solution.py:274
  783.9 248.3 %reduce-scatter.11.cloned.1.call-start = ((), (), s32[]{:S(2)}) async-start(), calls=%async_computation.14 | async-start | bytes 2228224 | tf_op jit(solution)/shard_map/reduce_scatter | solution.py:277
  789.6 350.7 %reduce-scatter.15.cloned.1.call-start = ((), (), s32[]{:S(2)}) async-start(), calls=%async_computation.16 | async-start | bytes 8912896 | tf_op jit(solution)/shard_map/reduce_scatter | solution.py:176
  804.5 444.8 %reduce-scatter.17.cloned.1.call-start = ((), (), s32[]{:S(2)}) async-start(), calls=%async_computation.17 | async-start | bytes 8912896 | tf_op jit(solution)/shard_map/reduce_scatter | solution.py:179
  822.6 481.7 %all-reduce.27.cloned.1.call-start = ((), (), s32[]{:S(2)}) async-start(), calls=%async_computation.21 | async-start | bytes 3145728 | tf_op jit(solution)/shard_map/psum | solution.py:300
  1249.3 25.8 %copy-start.4 = (f32[784,1024]{1,0:T(8,128)S(1)}, f32[784,1024]{1,0:T(8,128)}, u32[]{:S(2)}) copy-start(f32[784,1024]{1,0:T(8,128)} %copy-done.3) | copy-start | bytes 9633796
  1249.3 25.8 %copy-start.26 = (f32[784]{0:T(1024)S(1)}, f32[784]{0:T(1024)}, u32[]{:S(2)}) copy-start(f32[784]{0:T(1024)} %copy-done.25) | copy-start | bytes 9412
  (34 other events, 170.1 us)
Sparse Core Ops, SparseCore 0:
  10.2 44.2 all-gather.11
  56.7 40.1 all-gather.13
  99.0 40.1 all-gather.15
  141.2 44.4 all-gather.23
  187.7 45.6 all-gather.25
  235.4 41.3 all-gather.17
  279.0 73.6 all-gather.19
  354.9 73.1 all-gather.21
  618.6 154.2 all-reduce.24
  777.0 61.6 reduce-scatter.12
  842.4 60.8 reduce-scatter.6
  907.4 60.5 reduce-scatter.8
  971.7 60.4 reduce-scatter.10
  1036.7 103.6 reduce-scatter.14
  1144.8 104.4 reduce-scatter.16
  1252.0 52.3 all-reduce.26
where the time goes:
time: 1330 us; the launch traced here: 1320 us
  waiting for transfers between devices  685 us (52%)
  matrix products  324 us (24%)
  blocking collectives  150 us (11%)
  other arithmetic  73.4 us (6%)
  local copies, waits for them, and re-layouts  69.9 us (5%)
  between operations  17.4 us (1%)
    unnamed x2, blocking collectives  126 us
    unnamed x17, waiting for transfers between devices  124 us
    reduce_scatter x1, waiting for transfers between devices, on_device(): lax.psum_scatter(down_wgrad.astype(jnp.bfloat16), 'fsdp', scatter_dimensi...  109 us
    reduce_scatter x1, waiting for transfers between devices, on_device(): lax.psum_scatter(up_wgrad.astype(jnp.bfloat16), 'fsdp', scatter_dimension...  108 us
    reduce_scatter x1, waiting for transfers between devices, on_device(): lax.psum_scatter(key_wgrad.astype(jnp.bfloat16), 'fsdp', scatter_dimensio...  64.7 us
    reduce_scatter x1, waiting for transfers between devices, on_device(): lax.psum_scatter(value_wgrad.astype(jnp.bfloat16), 'fsdp', scatter_dimens...  64.2 us
    all_gather x1, waiting for transfers between devices, gather_feed(): lax.all_gather(shards[1], 'fsdp', axis=0, tiled=True)  62.1 us
    dot_general x1, matrix products, on_device(): jnp.einsum('cqhd,ckhd->cqhk', grad_heads, value_heads_all, preferred_elem...  44 us
  transfers between devices with their start and end apart: 16, of which 13 were waited for; matrix products, arithmetic and copies ran while one was open for 20% of the time, Pallas kernels for 0%

commit v1 on v0

--- a/solution.py
+++ b/solution.py
@@ -1,10 +1,15 @@
+import functools
+
 import jax
 import jax.numpy as jnp
 from jax import lax
+from jax.experimental import pallas as pl
+from jax.experimental.pallas import tpu as pltpu
 from jax.sharding import PartitionSpec as P
 
 HEADS = 16
 HDIM = 64
+MESH = pl.DeviceIdType.MESH
 
 
 epsilon = 1e-05
@@ -45,7 +50,7 @@
     )
 
 
-def on_device(
+def plain_device(
     activations,
     cotangent,
     query_weight,
@@ -328,9 +333,452 @@
     )
 
 
+def place():
+    f = lax.axis_index("fsdp"); y = lax.axis_index("ctx")
+    return f // 4, (f // 2) % 2, f % 2, y
+
+def greet(z, x, c, y, depth):
+    barrier = pltpu.get_barrier_semaphore()
+    def one(dz, dx, dc, dy):
+        pl.semaphore_signal(barrier, inc=1, device_id=(dz * 4 + dx * 2 + dc, dy), device_id_type=MESH)
+    for k in range(1, depth):
+        one((z + k) % depth, x, c, y)
+    one(z, 1 - x, c, y); one(z, x, 1 - c, y); one(z, x, c, 1 - y)
+    pl.semaphore_wait(barrier, depth + 2)
+
+class Gather:
+    def __init__(self, depth, chunks, ins, outs, sems, where):
+        self.depth, self.chunks, self.ins, self.outs = depth, chunks, ins, outs
+        self.zs, self.zr, self.xs, self.xr, self.ys, self.yr, self.cs, self.cr, self.loc = sems
+        self.where = where
+    def src(self, ch, half):
+        t, r0, h, both = self.chunks[ch]
+        if not both: return self.ins[t].at[pl.ds(r0, h)]
+        h2 = h // 2
+        return self.ins[t].at[pl.ds(pl.multiple_of(r0 + half * h2, 16), h2)]
+    def dst(self, ch, dz, dx, dc, half):
+        t, r0, h, both = self.chunks[ch]
+        full = self.ins[t].shape[0]
+        start = (dz * 4 + dx * 2 + dc) * full + r0
+        if not both: return self.outs[t].at[pl.ds(pl.multiple_of(start, 16), h)]
+        h2 = h // 2
+        return self.outs[t].at[pl.ds(pl.multiple_of(start + half * h2, 16), h2)]
+    def copy(self, src, dst, s, r, dz, dx, dc, dy):
+        return pltpu.make_async_remote_copy(src_ref=src, dst_ref=dst, send_sem=s, recv_sem=r,
+            device_id=(dz * 4 + dx * 2 + dc, dy), device_id_type=MESH)
+    def zz(self, j):
+        return (self.where[0] - j + self.depth) % self.depth
+    def zmove(self, ch, k, recv=False):
+        z, x, c, y = self.where
+        if recv:
+            d = self.dst(ch, self.zz(k), x, c, y)
+            return self.copy(d, d, self.zs.at[ch, k], self.zr.at[ch, k], z, x, 1 - c, y)
+        return self.copy(self.src(ch, y), self.dst(ch, z, x, c, y), self.zs.at[ch, k], self.zr.at[ch, k], (z + k) % self.depth, x, c, y)
+    def xmove(self, ch, j, recv=False):
+        z, x, c, y = self.where
+        d = self.dst(ch, self.zz(j), 1 - x if recv else x, c, y)
+        s = self.src(ch, y) if (j == 0 and not recv) else d
+        return self.copy(s, d, self.xs.at[ch, j], self.xr.at[ch, j], z, 1 - x, c, y)
+    def ymove(self, ch, i, j, recv=False):
+        z, x, c, y = self.where
+        d = self.dst(ch, self.zz(j), x if i == 0 else 1 - x, c, 1 - y if recv else y)
+        n = i * self.depth + j
+        return self.copy(d, d, self.ys.at[ch, n], self.yr.at[ch, n], z, x, c, 1 - y)
+    def cmove(self, ch, i, j, other, recv=False):
+        z, x, c, y = self.where
+        half = 1 - y if other else y
+        d = self.dst(ch, self.zz(j), x if i == 0 else 1 - x, 1 - c if recv else c, half)
+        s = self.src(ch, half) if (i == 0 and j == 0 and not recv) else d
+        n = (i * self.depth + j) + (2 * self.depth if other else 0)
+        return self.copy(s, d, self.cs.at[ch, n], self.cr.at[ch, n], z, x, 1 - c, y)
+    def own(self, ch):
+        z, x, c, y = self.where
+        t, r0, h, both = self.chunks[ch]
+        full = self.ins[t].shape[0]
+        return pltpu.make_async_copy(self.ins[t].at[pl.ds(r0, h)],
+            self.outs[t].at[pl.ds(pl.multiple_of((z * 4 + x * 2 + c) * full + r0, 16), h)], self.loc.at[ch])
+    def begin(self, ch):
+        for k in range(1, self.depth): self.zmove(ch, k).start()
+        self.xmove(ch, 0).start()
+        self.cmove(ch, 0, 0, False).start()
+        if self.chunks[ch][3]: self.cmove(ch, 0, 0, True).start()
+        self.own(ch).start()
+    def zstage(self, ch):
+        for k in range(1, self.depth):
+            self.zmove(ch, k, True).wait_recv()
+            self.xmove(ch, k).start()
+            if self.chunks[ch][3]: self.ymove(ch, 0, k).start()
+            self.cmove(ch, 0, k, False).start()
+    def xstage(self, ch):
+        for j in range(self.depth):
+            self.xmove(ch, j, True).wait_recv()
+            if self.chunks[ch][3]: self.ymove(ch, 1, j).start()
+            self.cmove(ch, 1, j, False).start()
+    def ystage(self, ch):
+        if not self.chunks[ch][3]: return
+        for i in range(2):
+            for j in range(1 - i, self.depth):
+                self.ymove(ch, i, j, True).wait_recv()
+                self.cmove(ch, i, j, True).start()
+    def arrived(self, ch):
+        for i in range(2):
+            for j in range(self.depth):
+                self.cmove(ch, i, j, False, True).wait_recv()
+                if self.chunks[ch][3]: self.cmove(ch, i, j, True, True).wait_recv()
+        self.own(ch).wait()
+    def sent(self, ch):
+        both = self.chunks[ch][3]
+        for k in range(1, self.depth): self.zmove(ch, k).wait_send()
+        for j in range(self.depth): self.xmove(ch, j).wait_send()
+        for i in range(2):
+            for j in range(self.depth):
+                self.cmove(ch, i, j, False).wait_send()
+                if both:
+                    self.cmove(ch, i, j, True).wait_send()
+                    if i or j: self.ymove(ch, i, j).wait_send()
+
+def gather_sems(depth, n):
+    S = pltpu.SemaphoreType.DMA
+    return [S((n, depth)), S((n, depth)), S((n, depth)), S((n, depth)), S((n, 2 * depth)), S((n, 2 * depth)), S((n, 4 * depth)), S((n, 4 * depth)), S((n,))]
+
+def ag_kernel(depth, n, chunks, ahead, lag, *refs):
+    ins = refs[:n]; x_in = refs[n]
+    outs = refs[n + 1:2 * n + 1]; x_out = refs[2 * n + 1]
+    sems = refs[2 * n + 2:2 * n + 11]; ys, yr = refs[2 * n + 11:]
+    z, x, c, y = place()
+    g = Gather(depth, chunks, ins, outs, sems, (z, x, c, y))
+    greet(z, x, c, y, depth)
+    xw = g.copy(x_in, x_out, ys, yr, z, x, c, 1 - y)
+    xw.start()
+    N = len(chunks)
+    for ch in range(min(ahead, N)): g.begin(ch)
+    for s in range(N + 2 * lag):
+        if s < N:
+            g.zstage(s)
+            if s + ahead < N: g.begin(s + ahead)
+        if 0 <= s - lag < N: g.xstage(s - lag)
+        if 0 <= s - 2 * lag < N: g.ystage(s - 2 * lag)
+    xw.wait()
+    for ch in range(N): g.arrived(ch)
+    for ch in range(N): g.sent(ch)
+
+
+def gather_all(shards, x, chunks, depth=4, ahead=2, lag=1, cid=1):
+    n = len(shards)
+    S = pltpu.SemaphoreType.DMA
+    return pl.pallas_call(
+        functools.partial(ag_kernel, depth, n, chunks, ahead, lag),
+        out_shape=[jax.ShapeDtypeStruct((depth * 4 * s.shape[0],) + s.shape[1:], s.dtype) for s in shards] + [jax.ShapeDtypeStruct(x.shape, x.dtype)],
+        in_specs=[pl.BlockSpec(memory_space=pl.ANY)] * (n + 1),
+        out_specs=[pl.BlockSpec(memory_space=pl.ANY)] * (n + 1),
+        scratch_shapes=gather_sems(depth, len(chunks)) + [S, S],
+        compiler_params=pltpu.CompilerParams(collective_id=cid, has_side_effects=True),
+        name="weights_gather")(*shards, x)
+
+
+def rowwise(h, w, body):
+    wide = min(w, 1024 if w % 1024 == 0 else 512)
+    steps_w = w // wide
+    total = (h // 16) * steps_w
+    if total == 1:
+        body(pl.ds(0, 16), pl.ds(0, wide)); return
+    def one(i, _):
+        body(pl.ds(pl.multiple_of((i // steps_w) * 16, 16), 16), pl.ds(pl.multiple_of((i % steps_w) * wide, 128), wide))
+        return 0
+    lax.fori_loop(0, total, one, 0)
+
+class Scatter:
+    def __init__(self, depth, chunks, grads, outs, bufs, sems, where):
+        self.depth, self.chunks, self.grads, self.outs, self.bufs = depth, chunks, grads, outs, bufs
+        self.ls, self.cs, self.cr, self.xs, self.xr, self.zs, self.zr, self.ys, self.yr = sems
+        self.where = where
+    def piece(self, ch, dz, dx, dc):
+        t, k, r0, h = self.chunks[ch]
+        full = self.grads[t].shape[0] // (4 * self.depth)
+        return self.grads[t].at[pl.ds(pl.multiple_of((dz * 4 + dx * 2 + dc) * full + r0, 16), h)]
+    def copy(self, src, dst, s, r, dz, dx, dc, dy):
+        return pltpu.make_async_remote_copy(src_ref=src, dst_ref=dst, send_sem=s, recv_sem=r,
+            device_id=(dz * 4 + dx * 2 + dc, dy), device_id_type=MESH)
+    def zz(self, j): return (self.where[0] + j) % self.depth
+    def load(self, ch, i, j):
+        z, x, c, y = self.where; t, k = self.chunks[ch][:2]
+        return pltpu.make_async_copy(self.piece(ch, self.zz(j), x if i == 0 else 1 - x, c), self.bufs[t][0].at[k, i, j], self.ls.at[ch, i * self.depth + j])
+    def cmove(self, ch, i, j):
+        z, x, c, y = self.where; t, k = self.chunks[ch][:2]; n = i * self.depth + j
+        return self.copy(self.piece(ch, self.zz(j), x if i == 0 else 1 - x, 1 - c), self.bufs[t][1].at[k, i, j], self.cs.at[ch, n], self.cr.at[ch, n], z, x, 1 - c, y)
+    def xmove(self, ch, j):
+        z, x, c, y = self.where; t, k = self.chunks[ch][:2]
+        return self.copy(self.bufs[t][0].at[k, 1, j], self.bufs[t][2].at[k, j], self.xs.at[ch, j], self.xr.at[ch, j], z, 1 - x, c, y)
+    def zmove(self, ch, j):
+        z, x, c, y = self.where; t, k = self.chunks[ch][:2]
+        return self.copy(self.bufs[t][0].at[k, 0, j], self.bufs[t][3].at[k, j - 1], self.zs.at[ch, j], self.zr.at[ch, j], self.zz(j), x, c, y)
+    def ymove(self, ch):
+        z, x, c, y = self.where; t, k = self.chunks[ch][:2]
+        return self.copy(self.bufs[t][4].at[k], self.bufs[t][5].at[k], self.ys.at[ch], self.yr.at[ch], z, x, c, 1 - y)
+    def begin(self, ch):
+        for i in (1, 0):
+            for j in range(self.depth):
+                self.load(ch, i, j).start()
+                self.cmove(ch, i, j).start()
+    def cstage(self, ch):
+        t, k, r0, h = self.chunks[ch]; L, C = self.bufs[t][:2]; w = L.shape[-1]
+        for i in (1, 0):
+            for j in range(self.depth):
+                self.load(ch, i, j).wait(); self.cmove(ch, i, j).wait_recv()
+                def add(r, q):
+                    L[k, i, j, r, q] = L[k, i, j, r, q] + C[k, i, j, r, q]
+                rowwise(h, w, add)
+                if i == 1: self.xmove(ch, j).start()
+    def xstage(self, ch):
+        t, k, r0, h = self.chunks[ch]; L, C, X = self.bufs[t][:3]; w = L.shape[-1]
+        for j in list(range(1, self.depth)) + [0]:
+            self.xmove(ch, j).wait_recv()
+            def add(r, q):
+                L[k, 0, j, r, q] = L[k, 0, j, r, q] + X[k, j, r, q]
+            rowwise(h, w, add)
+            if j: self.zmove(ch, j).start()
+    def zstage(self, ch):
+        t, k, r0, h = self.chunks[ch]; L, C, X, Z, F, Y = self.bufs[t]; w = L.shape[-1]
+        for j in range(1, self.depth): self.zmove(ch, j).wait_recv()
+        def add(r, q):
+            tot = L[k, 0, 0, r, q].astype(jnp.float32)
+            for j in range(1, self.depth): tot = tot + Z[k, j - 1, r, q].astype(jnp.float32)
+            F[k, r, q] = tot.astype(jnp.bfloat16)
+        rowwise(h, w, add)
+        self.ymove(ch).start()
+    def ystage(self, ch):
+        t, k, r0, h = self.chunks[ch]; L, C, X, Z, F, Y = self.bufs[t]; w = L.shape[-1]
+        z, x, c, y = self.where
+        self.ymove(ch).wait_recv()
+        out = self.outs[t]
+        if out.shape[-1] == w:
+            def add(r, q):
+                out[pl.ds(pl.multiple_of(r0 + r.start, 16), 16), q] = F[k, r, q].astype(jnp.float32) + Y[k, r, q].astype(jnp.float32)
+            rowwise(h, w, add)
+        else:
+            part = w // 3
+            for n in range(3):
+                def lay(r, q, n=n):
+                    mine = F[k, r, n * part:(n + 1) * part].astype(jnp.float32)
+                    other = Y[k, r, n * part:(n + 1) * part].astype(jnp.float32)
+                    rr = pl.ds(pl.multiple_of(r0 + r.start, 16), 16)
+                    out[rr, 2 * n * part:(2 * n + 1) * part] = jnp.where(y == 0, mine, other)
+                    out[rr, (2 * n + 1) * part:(2 * n + 2) * part] = jnp.where(y == 0, other, mine)
+                rowwise(h, 128, lay)
+    def sent(self, ch):
+        for i in range(2):
+            for j in range(self.depth): self.cmove(ch, i, j).wait_send()
+        for j in range(self.depth):
+            self.xmove(ch, j).wait_send()
+            if j: self.zmove(ch, j).wait_send()
+        self.ymove(ch).wait_send()
+
+def scatter_scratch(depth, chunks, widths):
+    S = pltpu.SemaphoreType.DMA; n = len(chunks); out = []
+    for t, w in enumerate(widths):
+        mine = [c for c in chunks if c[0] == t]; m = len(mine); h = mine[0][3]
+        B = lambda *lead: pltpu.VMEM(lead + (h, w), jnp.bfloat16)
+        out += [B(m, 2, depth), B(m, 2, depth), B(m, depth), B(m, depth - 1), B(m), B(m)]
+    return out + [S((n, 2 * depth)), S((n, 2 * depth)), S((n, 2 * depth)), S((n, depth)), S((n, depth)), S((n, depth)), S((n, depth)), S((n,)), S((n,))]
+
+def rs_kernel(depth, n, chunks, lag, *refs):
+    grads, outs = refs[:n], refs[n:2 * n]
+    bufs = [refs[2 * n + 6 * t:2 * n + 6 * t + 6] for t in range(n)]
+    sems = refs[8 * n:8 * n + 9]
+    where = place()
+    s = Scatter(depth, chunks, grads, outs, bufs, sems, where)
+    greet(*where, depth)
+    N = len(chunks)
+    for ch in range(N): s.begin(ch)
+    for st in range(N + 3 * lag):
+        if st < N: s.cstage(st)
+        if 0 <= st - lag < N: s.xstage(st - lag)
+        if 0 <= st - 2 * lag < N: s.zstage(st - 2 * lag)
+        if 0 <= st - 3 * lag < N: s.ystage(st - 3 * lag)
+    for ch in range(N): s.sent(ch)
+
+def scatter_all(grads, chunks, wide, depth=4, lag=1, cid=2):
+    n = len(grads)
+    return pl.pallas_call(
+        functools.partial(rs_kernel, depth, n, chunks, lag),
+        out_shape=[jax.ShapeDtypeStruct((g.shape[0] // (4 * depth), g.shape[1] * (2 if t == wide else 1)), jnp.float32) for t, g in enumerate(grads)],
+        in_specs=[pl.BlockSpec(memory_space=pl.ANY)] * n,
+        out_specs=[pl.BlockSpec(memory_space=pltpu.VMEM)] * n,
+        scratch_shapes=scatter_scratch(depth, chunks, [g.shape[1] for g in grads]),
+        compiler_params=pltpu.CompilerParams(collective_id=cid, has_side_effects=True, vmem_limit_bytes=60 * 2 ** 20),
+        name="gradients_scatter")(*grads)
+
+
+DEPTH, BOTH = 4, 2
+
+
+def pack_small(vectors, up_bias, c):
+    rows = jnp.stack(vectors)
+    zero = jnp.zeros_like(rows)
+    rows = jnp.concatenate([jnp.where(c == 0, rows, zero), jnp.where(c == 0, zero, rows)], axis=1)
+    return jnp.concatenate([rows, up_bias.reshape(2, 128), jnp.zeros((6, 128), rows.dtype)], axis=0)
+
+
+def unpack_small(gathered):
+    blocks = gathered.astype(jnp.float32).reshape(-1, 2, 16, 128)
+    vectors = (blocks[:, 0, :8] + blocks[:, 1, :8]).transpose(1, 0, 2).reshape(8, -1)
+    return vectors, blocks[:, :, 8:10].reshape(-1)
+
+
+def pack_small_grads(vectors, up_grad):
+    parts = 4 * DEPTH
+    rows = jnp.stack(vectors).reshape(8, parts, 64).transpose(1, 0, 2)
+    rows = jnp.concatenate([rows, jnp.zeros_like(rows)], axis=2)
+    rows = jnp.concatenate([rows, up_grad.reshape(parts, 2, 128), jnp.zeros((parts, 6, 128), jnp.float32)], axis=1)
+    return rows.astype(jnp.bfloat16).reshape(parts * 16, 128)
+
+
+def swap(value):
+    return lax.ppermute(value, "ctx", [(0, 1), (1, 0)])
+
+
+def gather_chunks():
+    return (
+        (0, 0, 16, False),
+        (1, 0, 64, False),
+    ) + tuple((4, 64 * i, 64, True) for i in range(4)) + ((2, 0, 64, False),) + tuple(
+        (3, 16 * i, 16, False) for i in range(4)
+    )
+
+
+def scatter_chunks():
+    return ((0, 0, 0, 16),) + tuple((4, i, 64 * i, 64) for i in range(4)) + tuple(
+        (3, i, 16 * i, 16) for i in range(4)
+    ) + ((2, 0, 0, 64), (1, 0, 0, 64))
+
+
+def fast_device(
+    activations, cotangent, query_weight, key_weight, value_weight, output_weight, first_gain, first_shift,
+    query_bias, value_bias, output_bias, up_weight, down_weight, second_gain, second_shift, up_bias, down_bias,
+):
+    _, rows, width = activations.shape
+    half = width // 2
+    heads = half // HDIM
+    scaling = HDIM ** (-0.5)
+    y = lax.axis_index("ctx")
+    c = lax.axis_index("fsdp") % 2
+    f32, bf16 = jnp.float32, jnp.bfloat16
+
+    def mine(value):
+        return lax.dynamic_slice_in_dim(value, y * half, half, value.ndim - 1)
+
+    def others(value):
+        return lax.dynamic_slice_in_dim(value, (1 - y) * half, half, value.ndim - 1)
+
+    def both(own, other):
+        return jnp.where(y == 0, jnp.concatenate([own, other], -1), jnp.concatenate([other, own], -1))
+
+    small = pack_small(
+        (first_gain, first_shift, query_bias, value_bias, output_bias, second_gain, second_shift, down_bias), up_bias, c
+    )
+    own_qkv = jnp.concatenate([mine(query_weight), mine(key_weight), mine(value_weight)], axis=1)
+    x_own = activations[0]
+    all_small, all_qkv, all_out, all_up, all_down, x_other = gather_all(
+        (small, own_qkv, output_weight, up_weight, down_weight), x_own, gather_chunks()
+    )
+    vectors, full_up_bias = unpack_small(all_small)
+    gain_one, shift_one, full_query_bias, full_value_bias, full_output_bias, gain_two, shift_two, full_down_bias = vectors
+
+    token_rows = jnp.concatenate([x_own, x_other], axis=0).astype(f32)
+    normed_one = layer_norm(token_rows, gain_one, shift_one).astype(bf16)
+    bias = jnp.concatenate([mine(full_query_bias), jnp.zeros((half,), f32), mine(full_value_bias)])
+    qkv = (jnp.dot(normed_one, all_qkv, preferred_element_type=f32) + bias).astype(bf16)
+    queries, keys, values = [v.reshape(2 * rows, heads, HDIM) for v in jnp.split(qkv, 3, axis=1)]
+    scores = jnp.einsum("qhd,khd->hqk", queries, keys, preferred_element_type=f32) * scaling
+    top = jnp.max(scores, axis=-1, keepdims=True)
+    weights = jnp.exp(scores - top)
+    total = jnp.sum(weights, axis=-1, keepdims=True)
+    exact = jnp.einsum("hqk,khd->hqd", weights.astype(bf16), values, preferred_element_type=f32) / total
+    log_total = top + jnp.log(total)
+    attended_mine = exact.transpose(1, 0, 2).reshape(2 * rows, half).astype(bf16)
+    attended = both(attended_mine[:rows], swap(attended_mine[rows:]))
+
+    x_rows = x_own.astype(f32)
+    mid_rows = x_rows + jnp.dot(attended, all_out, preferred_element_type=f32) + full_output_bias
+    normed_two = layer_norm(mid_rows, gain_two, shift_two).astype(bf16)
+    pre_act = jnp.dot(normed_two, all_up, preferred_element_type=f32) + full_up_bias
+    hidden = gelu_act(pre_act).astype(bf16)
+    block_rows = mid_rows + jnp.dot(hidden, all_down, preferred_element_type=f32) + full_down_bias
+    block_out = block_rows.astype(bf16).reshape(activations.shape)
+
+    cot_rows = cotangent[0]
+    outer_grad = cot_rows.astype(f32)
+    down_wgrad = jnp.einsum("rf,rd->fd", hidden, cot_rows, preferred_element_type=f32).astype(bf16)
+    down_bgrad = jnp.sum(outer_grad, axis=0)
+    hidden_grad = jnp.einsum("rd,fd->rf", cot_rows, all_down, preferred_element_type=f32)
+    _, gelu_back = jax.vjp(gelu_act, pre_act)
+    pre_grad = gelu_back(hidden_grad)[0].astype(bf16)
+    up_wgrad = jnp.einsum("rd,rf->df", normed_two, pre_grad, preferred_element_type=f32).astype(bf16)
+    up_bgrad = jnp.sum(pre_grad.astype(f32), axis=0)
+    normed_two_grad = jnp.einsum("rf,df->rd", pre_grad, all_up, preferred_element_type=f32)
+    _, norm_two_back = jax.vjp(layer_norm, mid_rows, gain_two, shift_two)
+    mid_part, gain_two_grad, shift_two_grad = norm_two_back(normed_two_grad)
+    mid_grad = outer_grad + mid_part
+    branch_grad = mid_grad.astype(bf16)
+    output_wgrad = jnp.einsum("rd,re->de", attended, branch_grad, preferred_element_type=f32).astype(bf16)
+    output_bgrad = jnp.sum(branch_grad.astype(f32), axis=0)
+    attended_grad = jnp.einsum("re,de->rd", branch_grad, all_out, preferred_element_type=f32).astype(bf16)
+    grad_mine = jnp.concatenate([mine(attended_grad), swap(others(attended_grad))], axis=0)
+    grad_heads = grad_mine.reshape(2 * rows, heads, HDIM)
+    delta = jnp.einsum("qhd,hqd->hq", grad_heads.astype(f32), exact)[..., None]
+    scores = jnp.einsum("qhd,khd->hqk", queries, keys, preferred_element_type=f32) * scaling
+    probs = jnp.exp(scores - log_total)
+    prob_grad = jnp.einsum("qhd,khd->hqk", grad_heads, values, preferred_element_type=f32)
+    score_grad = (probs * (prob_grad - delta)).astype(bf16)
+    probs_low = probs.astype(bf16)
+    query_grad = jnp.einsum("hqk,khd->qhd", score_grad, keys, preferred_element_type=f32) * scaling
+    key_grad = jnp.einsum("hqk,qhd->khd", score_grad, queries, preferred_element_type=f32) * scaling
+    value_grad = jnp.einsum("hqk,qhd->khd", probs_low, grad_heads, preferred_element_type=f32)
+    qkv_grad = jnp.concatenate(
+        [v.astype(bf16).reshape(2 * rows, half) for v in (query_grad, key_grad, value_grad)], axis=1
+    )
+    qkv_wgrad = jnp.einsum("rd,re->de", normed_one, qkv_grad, preferred_element_type=f32).astype(bf16)
+    qkv_bgrad = jnp.sum(qkv_grad.astype(f32), axis=0)
+    nothing = jnp.zeros((half,), f32)
+    query_bgrad = both(qkv_bgrad[:half], nothing)
+    value_bgrad = both(qkv_bgrad[2 * half :], nothing)
+    normed_grad = jnp.einsum("re,de->rd", qkv_grad, all_qkv, preferred_element_type=f32)
+    normed_one_grad = normed_grad[:rows] + swap(normed_grad[rows:].astype(bf16)).astype(f32)
+    _, norm_one_back = jax.vjp(layer_norm, x_rows, gain_one, shift_one)
+    input_part, gain_one_grad, shift_one_grad = norm_one_back(normed_one_grad)
+    input_grad = (mid_grad + input_part).reshape(activations.shape)
+    small_grads = pack_small_grads(
+        (gain_one_grad, shift_one_grad, query_bgrad, value_bgrad, output_bgrad, gain_two_grad, shift_two_grad, down_bgrad),
+        up_bgrad,
+    )
+    own_small, own_qkv_grad, own_output, own_up, own_down = scatter_all(
+        (small_grads, qkv_wgrad, output_wgrad, up_wgrad, down_wgrad), scatter_chunks(), 1
+    )
+    return (
+        block_out,
+        input_grad,
+        own_qkv_grad[:, :width],
+        own_qkv_grad[:, width : 2 * width],
+        own_qkv_grad[:, 2 * width :],
+        own_output,
+        own_small[0, :64],
+        own_small[1, :64],
+        own_small[2, :64],
+        own_small[3, :64],
+        own_small[4, :64],
+        own_up,
+        own_down,
+        own_small[5, :64],
+        own_small[6, :64],
+        own_small[8:10].reshape(-1),
+        own_small[7, :64],
+    )
+
+
 def solution(mesh):
+    fits = mesh.shape["fsdp"] == 4 * DEPTH and mesh.shape["ctx"] == BOTH
     return jax.shard_map(
-        on_device,
+        fast_device if fits else plain_device,
         mesh=mesh,
         in_specs=(
             P("fsdp", "ctx", None),

time: 1330 us -> 709 us (0.53)
  waiting for transfers between devices: 685 us -> 39.1 us
  Pallas kernels: 0 us -> 271 us
  blocking collectives: 150 us -> 0 us
  local copies, waits for them, and re-layouts: 69.9 us -> 39.1 us
  other arithmetic: 73.4 us -> 49.7 us
  matrix products: 324 us -> 301 us
  between operations: 17.4 us -> 1.62 us
    reduce_scatter x6 -> x0, waiting for transfers between devices: 351 us -> none  [the longest x1 109 us: on_device(): lax.psum_scatter(down_wgrad.astype(jnp.bfloat16), 'fsdp', scatter_dimensi...]
    pallas_call x0 -> x2, Pallas kernels: none -> 271 us  [the longest x1 145 us: scatter_all(): pl.pallas_call(functools.partial(rs_kernel, depth, n, chunks, lag), out_s...]
    all_gather x8 -> x0, waiting for transfers between devices: 185 us -> none  [the longest x1 62.1 us: gather_feed(): lax.all_gather(shards[1], 'fsdp', axis=0, tiled=True)]
    unnamed x2 -> x0, blocking collectives: 126 us -> none
    unnamed x17 -> x0, waiting for transfers between devices: 124 us -> none
    ppermute x0 -> x3, waiting for transfers between devices: none -> 39.1 us  [swap(): return lax.ppermute(value, 'ctx', [(0, 1), (1, 0)])]
    another operation x2 -> x12, local copies, waits for them, and re-layouts: 28.4 us -> 3.93 us  [the longest x9 2.41 us: pack_small_grads(): rows = jnp.stack(vectors).reshape(8, parts, 64).transpose(1, 0, 2)]
    psum x1 -> x0, waiting for transfers between devices: 24.5 us -> none  [on_device(): lax.psum(attend_owned[0].astype(jnp.bfloat16), 'ctx').astype(jnp.float32)]
  transfers between devices with their start and end apart: 16 -> 3, of which waited for: 13 -> 2; matrix products, arithmetic and copies ran while one was open for 20% -> 5% of each run, Pallas kernels for 0% -> 0%
where the time goes in v1:
time: 709 us; the launch traced here: 704 us
  matrix products  301 us (42%)
  Pallas kernels  271 us (38%)
  other arithmetic  49.7 us (7%)
  local copies, waits for them, and re-layouts  39.1 us (6%)
  waiting for transfers between devices  39.1 us (6%)
    pallas_call x1, Pallas kernels, scatter_all(): pl.pallas_call(functools.partial(rs_kernel, depth, n, chunks, lag), out_s...  145 us
    pallas_call x1, Pallas kernels, gather_all(): pl.pallas_call(functools.partial(ag_kernel, depth, n, chunks, ahead, lag)...  125 us
    dot_general x1, matrix products, fast_device(): jnp.einsum('qhd,khd->hqk', grad_heads, values, preferred_element_type=f32)  46 us
    ppermute x3, waiting for transfers between devices, swap(): return lax.ppermute(value, 'ctx', [(0, 1), (1, 0)])  39.1 us
    dot_general x1, matrix products, fast_device(): jnp.einsum('hqk,khd->hqd', weights.astype(bf16), values, preferred_elemen...  31 us
    dot_general x1, matrix products, fast_device(): jnp.einsum('qhd,khd->hqk', queries, keys, preferred_element_type=f32)  30 us
    dot_general x1, matrix products, fast_device(): jnp.einsum('hqk,qhd->khd', probs_low, grad_heads, preferred_element_type=...  29.4 us
    reduce_sum x1, other arithmetic, fast_device(): total = jnp.sum(weights, axis=-1, keepdims=True)  26 us
  transfers between devices with their start and end apart: 3, of which 2 were waited for; matrix products, arithmetic and copies ran while one was open for 5% of the time, Pallas kernels for 0%

profile of v1, /device:TPU:0, one launch (start us, length us, event | category | flops | bytes accessed | tf_op | source)
XLA Modules:
  0.0 704.0 jit_solution(3227261501505767883)
XLA Ops:
  4.6 125.5 %weights_gather.1 = (bf16[256,128]{1,0:T(8,128)(2,1)}, bf16[1024,1536]{1,0:T(8,128)(2,1)}, bf16[1024,1024]{1,0:T(8,128)(2,1)}, bf16[1024,4096]{1,0:T(8,128)(2,1)...) custom-call(bf16[16,128]{1,0:T(8,128)(2,1)} %maximum_maximum_fusion.refs_0_, ...), custom_call_target="tpu_custom_call" | custom-call | tf_op jit(solution)/shard_map/weights_gather/pallas_call | solution.py:469
  134.2 7.7 %add_convert_fusion = bf16[1568,1536]{1,0:T(8,128)(2,1)S(1)} fusion(bf16[1024,1536]{1,0:T(8,128)(2,1)S(1)} %copy-done.48, f32[1536]{0:T(1024)S(1)} %pad_maximum_fusion.4, f32[1024]{0:T(1024)S(1)} %bitcast.174, f32[1024]{0:T(1024)S(1)} %bitcast.160, f32[1568]{0:T(1024)S(1)} %add_rsqrt_fusion, f32[1568]{0:T(1024)S(1)} %broadcast_multiply_fusion, ...), kind=kOutput, calls=%fused_computation.25 | convolution fusion | flops 4951769088 | bytes 11200768 | tf_op jit(solution)/shard_map/dot_general | solution.py:690
  141.9 2.3 fusion.65
  144.3 2.7 copy.69
  147.0 4.1 copy.70
  151.1 3.6 copy.68
  154.6 30.0 %multiply_reduce_fusion = (f32[8,1568]{1,0:T(8,128)S(1)}, f32[8,1568,1568]{1,2,0:T(8,128)}) fusion(bf16[1568,8,64]{0,2,1:T(8,128)(2,1)} %bitcast.138, bf16[1568,8,64]{0,2,1:T(8,128)(2,1)S(1)} %bitcast.136), kind=kOutput, calls=%fused_computation.6 | convolution fusion | flops 2556956416 | bytes 81937408 | tf_op jit(solution)/shard_map/qhd,khd->hqk/dot_general | solution.py:692
  184.6 26.0 %fusion = f32[8,1568]{1,0:T(8,128)S(1)} fusion(f32[8,1568,1568]{1,2,0:T(8,128)} %get-tuple-element.82, f32[8,1568]{1,0:T(8,128)S(1)} %get-tuple-element.81), kind=kLoop, calls=%fused_computation.3 | loop fusion | flops 58994432 | bytes 78776320 | tf_op jit(solution)/shard_map/reduce_sum | solution.py:695
  210.6 31.0 %fusion.28 = (bf16[1568,8,64]{0,2,1:T(8,128)(2,1)}, f32[8,1568,64]{1,2,0:T(8,128)}) fusion(f32[1568,8]{0,1:T(8,128)S(1)} %bitcast.153, bf16[1568,8,64]{0,2,1:T(8,128)(2,1)S(1)} %bitcast.141, f32[8,1568,1568]{1,2,0:T(8,128)} %get-tuple-element.82, f32[8,1568]{1,0:T(8,128)S(1)} %get-tuple-element.81), kind=kOutput, calls=%fused_computation.50 | convolution fusion | flops 2578243584 | bytes 85198848 | tf_op jit(solution)/shard_map/hqk,khd->hqd/dot_general | solution.py:696
  241.6 3.4 fusion.66
  245.1 2.3 copy.72
  253.2 15.1 %collective-permute-done = bf16[784,512]{1,0:T(8,128)(2,1)} collective-permute-done((bf16[784,512]{1,0:T(8,128)(2,1)}, bf16[784,512]{1,0:T(8,128)(2,1)}, u32[]{:S(2)}, u32[]{:S(2)}) %collective-permute-start) | collective-permute-done | bytes 802848 | tf_op jit(solution)/shard_map/ppermute | solution.py:637
  268.3 4.7 fusion.70
  273.6 10.1 %fusion.58 = f32[784,4096]{1,0:T(8,128)} fusion(bf16[1024,4096]{1,0:T(8,128)(2,1)S(1)} %bitcast.190, f32[784,1024]{1,0:T(8,128)S(1)} %get-tuple-element.86, f32[1024]{0:T(1024)S(1)} %bitcast.176, f32[1024]{0:T(1024)S(1)} %bitcast.164, f32[784]{0:T(1024)S(1)} %fusion.50, f32[784]{0:T(1024)S(1)} %broadcast_multiply_fusion.2), kind=kOutput, calls=%fused_computation.134 | convolution fusion | flops 6580682752 | bytes 24459392 | tf_op jit(solution)/shard_map/dot_general | solution.py:704
  283.7 16.8 %convolution_convert_fusion.1.refs_4_ = bf16[4096,1024]{1,0:T(8,128)(2,1)} fusion(bf16[1,784,1024]{2,1,0:T(8,128)(2,1)S(1)} %copy-done.11, f32[784,4096]{1,0:T(8,128)} %fusion.58, f32[4096]{0:T(1024)S(1)} %bitcast.168), kind=kOutput, calls=%fused_computation.31 | convolution fusion | flops 6612975616 | bytes 22855680 | tf_op jit(solution)/shard_map/rf,rd->fd/dot_general | solution.py:711
  300.4 21.5 %fusion.71 = (bf16[4096]{0:T(1024)(128)(2,1)S(1)}, bf16[784,4096]{1,0:T(8,128)(2,1)}) fusion(f32[784,4096]{1,0:T(8,128)} %fusion.58, f32[4096]{0:T(1024)S(1)} %bitcast.169, bf16[4096,1024]{1,0:T(8,128)(2,1)} %get-tuple-element.33, bf16[1,784,1024]{2,1,0:T(8,128)(2,1)S(1)} %copy-done.11), kind=kOutput, calls=%fused_computation.144 | convolution fusion | flops 6647312384 | bytes 29286400 | tf_op jit(solution)/shard_map/rd,fd->rf/dot_general | solution.py:713
  321.9 14.8 %fusion.38 = bf16[1,784,1024]{2,1,0:T(8,128)(2,1)} fusion(f32[784,1024]{1,0:T(8,128)S(1)} %get-tuple-element.86, f32[1024]{0:T(1024)S(1)} %bitcast.178, bf16[4096,1024]{1,0:T(8,128)(2,1)} %get-tuple-element.33, f32[784,4096]{1,0:T(8,128)} %fusion.58, f32[4096]{0:T(1024)S(1)} %bitcast.170), kind=kOutput, calls=%fused_computation.72 | convolution fusion | flops 6611189760 | bytes 26071040 | tf_op jit(solution)/shard_map/dot_general | solution.py:706
  336.7 10.4 %multiply_reduce_fusion.1 = (bf16[1024]{0:T(1024)(128)(2,1)S(1)}, f32[784]{0:T(1024)S(1)}, bf16[1024]{0:T(1024)(128)(2,1)S(1)}, f32[784,1024]{1,0:T(8,128)S(1)}) fusion(f32[784,1024]{1,0:T(8,128)S(1)} %get-tuple-element.86, f32[784]{0:T(1024)S(1)} %fusion.50, f32[784]{0:T(1024)S(1)} %broadcast_multiply_fusion.2, f32[1024]{0:T(1024)S(1)} %bitcast.165, ...), kind=kOutput, calls=%fused_computation.61 | convolution fusion | flops 6583088128 | bytes 21251264 | tf_op jit(solution)/shard_map/rf,df->rd/dot_general | solution.py:718
  353.9 12.2 %convolution_convert_fusion.refs_3_ = bf16[1024,4096]{1,0:T(8,128)(2,1)} fusion(bf16[784,4096]{1,0:T(8,128)(2,1)S(1)} %bitcast.192, f32[784,1024]{1,0:T(8,128)S(1)} %get-tuple-element.86, f32[1024]{0:T(1024)S(1)} %bitcast.177, f32[1024]{0:T(1024)S(1)} %bitcast.167, f32[784]{0:T(1024)S(1)} %fusion.50, f32[784]{0:T(1024)S(1)} %broadcast_multiply_fusion.2), kind=kOutput, calls=%fused_computation.30 | convolution fusion | flops 6584877056 | bytes 18036864 | tf_op jit(solution)/shard_map/rd,rf->df/dot_general | solution.py:716
  367.4 5.7 convolution_convert_fusion.3.refs_2_
  375.8 2.6 fusion.27
  378.3 29.4 %fusion.34 = bf16[8,64,1568]{2,1,0:T(8,128)(2,1)} fusion(bf16[1568,8,64]{0,2,1:T(8,128)(2,1)S(1)} %bitcast.134, f32[8,1568,1568]{1,2,0:T(8,128)} %get-tuple-element.82, f32[8,1568]{1,0:T(8,128)S(1)} %copy-done.6), kind=kOutput, calls=%fused_computation.68 | convolution fusion | flops 2577440768 | bytes 81937408 | tf_op jit(solution)/shard_map/hqk,qhd->khd/dot_general | solution.py:736
  407.7 46.0 %multiply_convert_fusion = bf16[8,1568,1568]{1,2,0:T(8,128)(2,1)} fusion(f32[8,1568,1568]{1,2,0:T(8,128)} %get-tuple-element.82, bf16[1568,8,64]{0,2,1:T(8,128)(2,1)S(1)} %bitcast.135, bf16[1568,8,64]{0,2,1:T(8,128)(2,1)} %bitcast.140, f32[8,1568]{1,0:T(8,128)S(1)} %fusion.27, f32[8,1568]{1,0:T(8,128)S(1)} %copy-done.6), kind=kOutput, calls=%fused_computation | convolution fusion | flops 2615975936 | bytes 121325568 | tf_op jit(solution)/shard_map/qhd,khd->hqk/dot_general | solution.py:731
  453.7 20.1 %multiply_convert_fusion.2 = bf16[8,64,1568]{2,1,0:T(8,128)(2,1)} fusion(bf16[1568,8,64]{0,2,1:T(8,128)(2,1)S(1)} %bitcast.139, bf16[8,1568,1568]{1,2,0:T(8,128)(2,1)} %multiply_convert_fusion), kind=kOutput, calls=%fused_computation.51 | convolution fusion | flops 2519236608 | bytes 42549248 | tf_op jit(solution)/shard_map/hqk,qhd->khd/dot_general | solution.py:735
  473.8 17.7 %multiply_convert_fusion.3 = bf16[8,64,1568]{2,1,0:T(8,128)(2,1)} fusion(bf16[1568,8,64]{0,2,1:T(8,128)(2,1)S(1)} %bitcast.137, bf16[8,1568,1568]{1,2,0:T(8,128)(2,1)} %multiply_convert_fusion), kind=kOutput, calls=%fused_computation.52 | convolution fusion | flops 2519236608 | bytes 42549248 | tf_op jit(solution)/shard_map/hqk,khd->qhd/dot_general | solution.py:734
  491.5 2.9 convert_reduce_fusion
  494.4 10.2 %fusion.57 = f32[1568,1024]{1,0:T(8,128)} fusion(bf16[1024,1536]{1,0:T(8,128)(2,1)} %get-tuple-element.30, bf16[1568,512]{0,1:T(8,128)(2,1)S(1)} %bitcast.145, bf16[1568,512]{0,1:T(8,128)(2,1)S(1)} %bitcast.149, bf16[1568,512]{0,1:T(8,128)(2,1)S(1)} %bitcast.152), kind=kOutput, calls=%fused_computation.133 | convolution fusion | flops 4946952192 | bytes 14385152 | tf_op jit(solution)/shard_map/re,de->rd/dot_general | solution.py:745
  508.8 11.0 %convolution_convert_fusion.2.refs_1_ = bf16[1024,1536]{1,0:T(8,128)(2,1)} fusion(bf16[1568,512]{0,1:T(8,128)(2,1)S(1)} %bitcast.146, bf16[1568,512]{0,1:T(8,128)(2,1)} %bitcast.148, bf16[1568,512]{0,1:T(8,128)(2,1)} %bitcast.151, f32[1024]{0:T(1024)S(1)} %bitcast.175, f32[1024]{0:T(1024)S(1)} %bitcast.161, f32[1568]{0:T(1024)S(1)} %copy-done.41, ...), kind=kOutput, calls=%fused_computation.46 | convolution fusion | flops 4962975744 | bytes 11194624 | tf_op jit(solution)/shard_map/rd,re->de/dot_general | solution.py:740
  519.8 24.0 %collective-permute-done.2 = bf16[784,1024]{1,0:T(8,128)(2,1)S(1)} collective-permute-done((bf16[784,1024]{1,0:T(8,128)(2,1)S(1)}, bf16[784,1024]{1,0:T(8,128)(2,1)S(1)}, u32[]{:S(2)}, u32[]{:S(2)}) %collective-permute-start.2) | collective-permute-done | bytes 1605664 | tf_op jit(solution)/shard_map/ppermute | solution.py:637
  546.4 145.3 %gradients_scatter.1 = (f32[16,128]{1,0:T(8,128)}, f32[64,3072]{1,0:T(8,128)}, f32[64,1024]{1,0:T(8,128)}, f32[64,4096]{1,0:T(8,128)}, f32[256,1024]{1,0:T(8,128)}) custom-call(bf16[256,128]{1,0:T(8,128)(2,1)} %bitcast.156, bf16[1024,1536]{1,0:T(8,128)(2,1)} %convolution_convert_fusion.2.refs_1_, bf16[1024,1024]{1,0:T(8,128)(2,1)} %convolution_convert_fusion.3.refs_2_, ...), custom_call_target="tpu_custom_call" | custom-call | tf_op jit(solution)/shard_map/gradients_scatter/pallas_call | solution.py:602
  694.6 3.3 fusion.63
  698.8 2.3 add_bitcast_fusion
  (189 shorter events, 37.9 us)
Async XLA Ops:
  0.7 129.5 %copy-start.2 = (bf16[1,784,1024]{2,1,0:T(8,128)(2,1)S(1)}, bf16[1,784,1024]{2,1,0:T(8,128)(2,1)}, u32[]{:S(2)}) copy-start(bf16[1,784,1024]{2,1,0:T(8,128)(2,1)} %param.17) | copy-start | bytes 4816900
  0.8 131.5 %copy-start.45 = (bf16[16]{0:T(256)(128)(2,1)}, bf16[16]{0:T(256)(128)(2,1)S(1)}, u32[]{:S(2)}) copy-start(bf16[16]{0:T(256)(128)(2,1)S(1)} %pad.29.clone) | copy-start | bytes 100
  132.3 9.6 %copy-start.35 = (f32[1568]{0:T(1024)}, f32[1568]{0:T(1024)S(1)}, u32[]{:S(2)}) copy-start(f32[1568]{0:T(1024)S(1)} %broadcast_multiply_fusion) | copy-start | bytes 18820
  133.3 8.6 %copy-start.40 = (f32[1568]{0:T(1024)}, f32[1568]{0:T(1024)S(1)}, u32[]{:S(2)}) copy-start(f32[1568]{0:T(1024)S(1)} %add_rsqrt_fusion) | copy-start | bytes 18820
  134.0 7.9 %copy-start.32 = (f32[1,8,128]{2,0,1:T(1,128)}, f32[1,8,128]{2,0,1:T(1,128)S(1)}, u32[]{:S(2)}) copy-start(f32[1,8,128]{2,0,1:T(1,128)S(1)} %get-tuple-element.68) | copy-start | bytes 12292
  134.0 7.9 %copy-start.42 = (f32[1,8,128]{2,0,1:T(1,128)}, f32[1,8,128]{2,0,1:T(1,128)S(1)}, u32[]{:S(2)}) copy-start(f32[1,8,128]{2,0,1:T(1,128)S(1)} %get-tuple-element.67) | copy-start | bytes 12292
  147.0 7.6 %copy-start.7 = (bf16[1568,512]{0,1:T(8,128)(2,1)}, bf16[1568,512]{0,1:T(8,128)(2,1)S(1)}, u32[]{:S(2)}) copy-start(bf16[1568,512]{0,1:T(8,128)(2,1)S(1)} %copy.69) | copy-start | bytes 4816900
  184.6 26.0 %copy-start.10 = (bf16[1568,512]{0,1:T(8,128)(2,1)S(1)}, bf16[1568,512]{0,1:T(8,128)(2,1)}, u32[]{:S(2)}) copy-start(bf16[1568,512]{0,1:T(8,128)(2,1)} %copy.70) | copy-start | bytes 4816900
  210.6 41.9 %copy-start.16 = (f32[8,1568]{1,0:T(8,128)}, f32[8,1568]{1,0:T(8,128)S(1)}, u32[]{:S(2)}) copy-start(f32[8,1568]{1,0:T(8,128)S(1)} %fusion) | copy-start | bytes 150532
  241.6 6.6 copy-start.11
  247.4 20.9 %collective-permute-start = (bf16[784,512]{1,0:T(8,128)(2,1)}, bf16[784,512]{1,0:T(8,128)(2,1)}, u32[]{:S(2)}, u32[]{:S(2)}) collective-permute-start(bf16[784,512]{1,0:T(8,128)(2,1)} %copy.72), channel_id=1, source_target_pairs={{0,1},{1,0},{2,3},{3,2},{4,5},{5,4},{6,7},{7,6},{8,9},{9,8},{10,11... | collective-permute-start | bytes 2408456 | tf_op jit(solution)/shard_map/ppermute | solution.py:637
  249.2 23.8 %copy-start.28 = (f32[784]{0:T(1024)}, f32[784]{0:T(1024)S(1)}, u32[]{:S(2)}) copy-start(f32[784]{0:T(1024)S(1)} %broadcast_multiply_fusion.1) | copy-start | bytes 9412
  251.9 21.1 %copy-start.30 = (f32[784]{0:T(1024)}, f32[784]{0:T(1024)S(1)}, u32[]{:S(2)}) copy-start(f32[784]{0:T(1024)S(1)} %fusion.29) | copy-start | bytes 9412
  300.4 21.5 %copy-start.44 = (f32[1,8,128]{2,0,1:T(1,128)S(1)}, f32[1,8,128]{2,0,1:T(1,128)}, u32[]{:S(2)}) copy-start(f32[1,8,128]{2,0,1:T(1,128)} %get-tuple-element.62) | copy-start | bytes 12292
  348.2 5.6 slice-start.4
  353.3 14.2 %copy-start.22 = (bf16[784,1024]{1,0:T(8,128)(2,1)S(1)}, bf16[784,1024]{1,0:T(8,128)(2,1)}, u32[]{:S(2)}) copy-start(bf16[784,1024]{1,0:T(8,128)(2,1)} %copy-done.21) | copy-start | bytes 4816900
  353.3 19.9 %collective-permute-start.1 = (bf16[784,512]{1,0:T(8,128)(2,1)S(1)}, bf16[784,512]{1,0:T(8,128)(2,1)}, u32[]{:S(2)}, u32[]{:S(2)}) collective-permute-start(bf16[784,512]{1,0:T(8,128)(2,1)S(1)} %get-tuple-element.57), channel_id=1, source_target_pairs={{0,1},{1,0},{2,3},{3,2},{4,5},{5,4},{6,7},{7,6},{8,9},{9,8},{10,11... | collective-permute-start | bytes 2408456 | tf_op jit(solution)/shard_map/ppermute | solution.py:637
  407.7 46.0 %copy-start.9 = (bf16[1568,512]{0,1:T(8,128)(2,1)S(1)}, bf16[1568,512]{0,1:T(8,128)(2,1)}, u32[]{:S(2)}) copy-start(bf16[1568,512]{0,1:T(8,128)(2,1)} %copy.68) | copy-start | bytes 4816900
  453.7 20.1 %copy-start.8 = (bf16[1568,512]{0,1:T(8,128)(2,1)S(1)}, bf16[1568,512]{0,1:T(8,128)(2,1)}, u32[]{:S(2)}) copy-start(bf16[1568,512]{0,1:T(8,128)(2,1)} %copy-done.7) | copy-start | bytes 4816900
  473.8 17.7 %copy-start.13 = (bf16[8,64,1568]{2,1,0:T(8,128)(2,1)S(1)}, bf16[8,64,1568]{2,1,0:T(8,128)(2,1)}, u32[]{:S(2)}) copy-start(bf16[8,64,1568]{2,1,0:T(8,128)(2,1)} %fusion.34) | copy-start | bytes 4816900
  494.4 10.3 %copy-start.47 = (pred[1024]{0:T(1024)(128)(4,1)S(1)}, pred[1024]{0:T(1024)(128)(4,1)}, u32[]{:S(2)}) copy-start(pred[1024]{0:T(1024)(128)(4,1)} %constant.72.clone.1) | copy-start | bytes 3076
  504.8 39.0 %slice-start = ((s8[6422528]{0:T(1024)(128)(4,1)}), s8[4194304]{0:T(1024)(128)(4,1)S(1)}, s32[]{:S(2)}) async-start(s8[6422528]{0:T(1024)(128)(4,1)} %bitcast.142), calls=%async_computation | async-start | bytes 8388608
  507.2 36.7 %slice-start.1 = ((s8[6422528]{0:T(1024)(128)(4,1)}), s8[2228224]{0:T(1024)(128)(4,1)S(1)}, s32[]{:S(2)}) async-start(s8[6422528]{0:T(1024)(128)(4,1)} %bitcast.142), calls=%async_computation.1 | async-start | bytes 4456448
  507.2 36.7 %copy-start.29 = (f32[784]{0:T(1024)S(1)}, f32[784]{0:T(1024)}, u32[]{:S(2)}) copy-start(f32[784]{0:T(1024)} %copy-done.28) | copy-start | bytes 9412
  507.2 36.7 %copy-start.34 = (f32[784]{0:T(1024)S(1)}, f32[784]{0:T(1024)}, u32[]{:S(2)}) copy-start(f32[784]{0:T(1024)} %fusion.51) | copy-start | bytes 9412
  507.2 36.7 %collective-permute-start.2 = (bf16[784,1024]{1,0:T(8,128)(2,1)S(1)}, bf16[784,1024]{1,0:T(8,128)(2,1)S(1)}, u32[]{:S(2)}, u32[]{:S(2)}) collective-permute-start(bf16[784,1024]{1,0:T(8,128)(2,1)S(1)} %slice.143), channel_id=1, source_target_pairs={{0,1},{1,0},{2,3},{3,2},{4,5},{5,4},{6,7},{7,6},{8,9},{9,8},{10,11... | collective-permute-start | bytes 4816904 | tf_op jit(solution)/shard_map/ppermute | solution.py:637
  519.8 25.8 %copy-start.39 = (bf16[1,16,64]{2,1,0:T(8,128)(2,1)S(1)}, bf16[1,16,64]{2,1,0:T(8,128)(2,1)}, u32[]{:S(2)}) copy-start(bf16[1,16,64]{2,1,0:T(8,128)(2,1)} %stack.67) | copy-start | bytes 6148
  519.8 25.8 %copy-start.38 = (bf16[1,16,64]{2,1,0:T(8,128)(2,1)S(1)}, bf16[1,16,64]{2,1,0:T(8,128)(2,1)}, u32[]{:S(2)}) copy-start(bf16[1,16,64]{2,1,0:T(8,128)(2,1)} %stack.69) | copy-start | bytes 6148
  519.8 25.8 %copy-start.37 = (bf16[1,16,64]{2,1,0:T(8,128)(2,1)S(1)}, bf16[1,16,64]{2,1,0:T(8,128)(2,1)}, u32[]{:S(2)}) copy-start(bf16[1,16,64]{2,1,0:T(8,128)(2,1)} %stack.70) | copy-start | bytes 6148
  519.8 25.9 %copy-start.46 = (bf16[16]{0:T(256)(128)(2,1)S(1)}, bf16[16]{0:T(256)(128)(2,1)}, u32[]{:S(2)}) copy-start(bf16[16]{0:T(256)(128)(2,1)} %copy-done.45) | copy-start | bytes 100
  546.4 148.1 %copy-start.31 = (f32[784]{0:T(1024)S(1)}, f32[784]{0:T(1024)}, u32[]{:S(2)}) copy-start(f32[784]{0:T(1024)} %copy-done.30) | copy-start | bytes 9412
  546.4 148.1 %copy-start.20 = (bf16[784,1024]{1,0:T(8,128)(2,1)S(1)}, bf16[784,1024]{1,0:T(8,128)(2,1)}, u32[]{:S(2)}) copy-start(bf16[784,1024]{1,0:T(8,128)(2,1)} %copy-done.19) | copy-start | bytes 4816900
  (27 other events, 86.6 us)

commit v2 on v1

--- a/solution.py
+++ b/solution.py
@@ -609,6 +609,170 @@
         name="gradients_scatter")(*grads)
 
 
+NT = (((1,), (1,)), ((), ()))
+NN = (((1,), (0,)), ((), ()))
+
+
+def attend_kernel(block_rows, qkv, attended, inverse, weights_out, values_ones, kept, sem):
+    length = qkv.shape[0]
+    half = qkv.shape[1] // 3
+    blocks, pairs = length // block_rows, half // 128
+    low_lanes = lax.broadcasted_iota(jnp.int32, (block_rows, 128), 1) < HDIM
+
+    def out(pair, block, head, slot):
+        rows = pl.ds(pl.multiple_of(block * block_rows, 16), block_rows)
+        return pltpu.make_async_copy(kept.at[slot, head], weights_out.at[2 * pair + head, rows], sem.at[slot, head])
+
+    values_ones[:, 128:] = jnp.ones((length, 128), jnp.bfloat16)
+
+    def one_pair(pair, _):
+        at = pl.multiple_of(pair * 128, 128)
+        values_ones[:, :128] = qkv[:, pl.ds(2 * half + at, 128)]
+
+        def one_block(block, _):
+            turn = pair * blocks + block
+            slot = turn % 2
+
+            @pl.when(turn > 1)
+            def _():
+                for head in range(2):
+                    out(0, 0, head, slot).wait()
+
+            rows = pl.ds(pl.multiple_of(block * block_rows, 16), block_rows)
+            queries = qkv[rows, pl.ds(at, 128)] * jnp.bfloat16(HDIM**-0.5)
+            keys = qkv[:, pl.ds(half + at, 128)]
+            values = values_ones[...]
+            parts = []
+            for head in range(2):
+                masked = jnp.where(low_lanes == (head == 0), queries, jnp.zeros_like(queries))
+                scores = lax.dot_general(masked, keys, NT, preferred_element_type=jnp.float32)
+                top = jnp.max(scores, axis=1, keepdims=True)
+                weights = jnp.exp(scores - top).astype(jnp.bfloat16)
+                kept[slot, head] = weights
+                summed = lax.dot_general(weights, values, NN, preferred_element_type=jnp.float32)
+                parts.append((summed[:, :128], 1.0 / summed[:, 128:]))
+            (low, low_inverse), (high, high_inverse) = parts
+            scale = jnp.where(low_lanes, low_inverse, high_inverse)
+            attended[rows, pl.ds(at, 128)] = (jnp.where(low_lanes, low, high) * scale).astype(jnp.bfloat16)
+            inverse[rows, pl.ds(at, 128)] = scale
+            for head in range(2):
+                out(pair, block, head, slot).start()
+            return 0
+
+        lax.fori_loop(0, blocks, one_block, 0)
+        return 0
+
+    lax.fori_loop(0, pairs, one_pair, 0)
+    for slot in range(2):
+        for head in range(2):
+            out(0, 0, head, slot).wait()
+
+
+def attend(qkv, block_rows):
+    length, wide = qkv.shape
+    half = wide // 3
+    whole = pl.BlockSpec(memory_space=pltpu.VMEM)
+    return pl.pallas_call(
+        functools.partial(attend_kernel, block_rows),
+        out_shape=[
+            jax.ShapeDtypeStruct((length, half), jnp.bfloat16),
+            jax.ShapeDtypeStruct((length, half), jnp.float32),
+            jax.ShapeDtypeStruct((half // HDIM, length, length), jnp.bfloat16),
+        ],
+        in_specs=[whole],
+        out_specs=[whole, whole, pl.BlockSpec(memory_space=pl.ANY)],
+        scratch_shapes=[
+            pltpu.VMEM((length, 256), jnp.bfloat16),
+            pltpu.VMEM((2, 2, block_rows, length), jnp.bfloat16),
+            pltpu.SemaphoreType.DMA((2, 2)),
+        ],
+        compiler_params=pltpu.CompilerParams(vmem_limit_bytes=60 * 2**20),
+        name="attend",
+    )(qkv)
+
+
+def attend_back_kernel(block_rows, qkv, attended, inverse, grads, weights_in, out, key_sum, value_sum, kept, sem):
+    length = qkv.shape[0]
+    half = qkv.shape[1] // 3
+    blocks, pairs = length // block_rows, half // 128
+    low_lanes = lax.broadcasted_iota(jnp.int32, (block_rows, 128), 1) < HDIM
+
+    def load(turn, head, slot):
+        rows = pl.ds(pl.multiple_of((turn % blocks) * block_rows, 16), block_rows)
+        return pltpu.make_async_copy(weights_in.at[2 * (turn // blocks) + head, rows], kept.at[slot, head], sem.at[slot, head])
+
+    for head in range(2):
+        load(0, head, 0).start()
+
+    def one_pair(pair, _):
+        at = pl.multiple_of(pair * 128, 128)
+
+        def one_block(block, _):
+            turn = pair * blocks + block
+            slot = turn % 2
+            for head in range(2):
+                load(turn, head, slot).wait()
+
+            @pl.when(turn + 1 < blocks * pairs)
+            def _():
+                for head in range(2):
+                    load(turn + 1, head, 1 - slot).start()
+
+            rows = pl.ds(pl.multiple_of(block * block_rows, 16), block_rows)
+            queries = qkv[rows, pl.ds(at, 128)] * jnp.bfloat16(HDIM**-0.5)
+            keys = qkv[:, pl.ds(half + at, 128)]
+            values = qkv[:, pl.ds(2 * half + at, 128)]
+            scaled = grads[rows, pl.ds(at, 128)].astype(jnp.float32) * inverse[rows, pl.ds(at, 128)]
+            product = scaled * attended[rows, pl.ds(at, 128)].astype(jnp.float32)
+            low = scaled.astype(jnp.bfloat16)
+            queries_t, low_t = queries.T, low.T
+            query_parts, key_parts, value_parts = [], [], []
+            for head in range(2):
+                own = low_lanes == (head == 0)
+                lanes = slice(HDIM * head, HDIM * head + HDIM)
+                masked = jnp.where(own, low, jnp.zeros_like(low))
+                prob_grad = lax.dot_general(masked, values, NT, preferred_element_type=jnp.float32)
+                delta = jnp.sum(jnp.where(own, product, 0.0), axis=1, keepdims=True)
+                weights = kept[slot, head]
+                score_grad = (weights.astype(jnp.float32) * (prob_grad - delta)).astype(jnp.bfloat16)
+                query_parts.append(lax.dot_general(score_grad, keys, NN, preferred_element_type=jnp.float32))
+                key_parts.append(lax.dot_general(queries_t[lanes], score_grad, NN, preferred_element_type=jnp.float32))
+                value_parts.append(lax.dot_general(low_t[lanes], weights, NN, preferred_element_type=jnp.float32))
+            query_grad = jnp.where(low_lanes, query_parts[0], query_parts[1]) * HDIM**-0.5
+            out[rows, pl.ds(at, 128)] = query_grad.astype(jnp.bfloat16)
+            key_part = jnp.concatenate(key_parts, axis=0)
+            value_part = jnp.concatenate(value_parts, axis=0)
+            key_sum[...] = jnp.where(block == 0, key_part, key_sum[...] + key_part)
+            value_sum[...] = jnp.where(block == 0, value_part, value_sum[...] + value_part)
+            return 0
+
+        lax.fori_loop(0, blocks, one_block, 0)
+        out[:, pl.ds(half + at, 128)] = key_sum[...].T.astype(jnp.bfloat16)
+        out[:, pl.ds(2 * half + at, 128)] = value_sum[...].T.astype(jnp.bfloat16)
+        return 0
+
+    lax.fori_loop(0, pairs, one_pair, 0)
+
+
+def attend_back(qkv, attended, inverse, grads, weights, block_rows):
+    length, wide = qkv.shape
+    whole = pl.BlockSpec(memory_space=pltpu.VMEM)
+    return pl.pallas_call(
+        functools.partial(attend_back_kernel, block_rows),
+        out_shape=jax.ShapeDtypeStruct((length, wide), jnp.bfloat16),
+        in_specs=[whole] * 4 + [pl.BlockSpec(memory_space=pl.ANY)],
+        out_specs=whole,
+        scratch_shapes=[
+            pltpu.VMEM((128, length), jnp.float32),
+            pltpu.VMEM((128, length), jnp.float32),
+            pltpu.VMEM((2, 2, block_rows, length), jnp.bfloat16),
+            pltpu.SemaphoreType.DMA((2, 2)),
+        ],
+        compiler_params=pltpu.CompilerParams(vmem_limit_bytes=60 * 2**20),
+        name="attend_back",
+    )(qkv, attended, inverse, grads, weights)
+
+
 DEPTH, BOTH = 4, 2
 
 
@@ -658,8 +822,6 @@
 ):
     _, rows, width = activations.shape
     half = width // 2
-    heads = half // HDIM
-    scaling = HDIM ** (-0.5)
     y = lax.axis_index("ctx")
     c = lax.axis_index("fsdp") % 2
     f32, bf16 = jnp.float32, jnp.bfloat16
@@ -688,14 +850,7 @@
     normed_one = layer_norm(token_rows, gain_one, shift_one).astype(bf16)
     bias = jnp.concatenate([mine(full_query_bias), jnp.zeros((half,), f32), mine(full_value_bias)])
     qkv = (jnp.dot(normed_one, all_qkv, preferred_element_type=f32) + bias).astype(bf16)
-    queries, keys, values = [v.reshape(2 * rows, heads, HDIM) for v in jnp.split(qkv, 3, axis=1)]
-    scores = jnp.einsum("qhd,khd->hqk", queries, keys, preferred_element_type=f32) * scaling
-    top = jnp.max(scores, axis=-1, keepdims=True)
-    weights = jnp.exp(scores - top)
-    total = jnp.sum(weights, axis=-1, keepdims=True)
-    exact = jnp.einsum("hqk,khd->hqd", weights.astype(bf16), values, preferred_element_type=f32) / total
-    log_total = top + jnp.log(total)
-    attended_mine = exact.transpose(1, 0, 2).reshape(2 * rows, half).astype(bf16)
+    attended_mine, inverse, weights = attend(qkv, rows)
     attended = both(attended_mine[:rows], swap(attended_mine[rows:]))
 
     x_rows = x_own.astype(f32)
@@ -724,19 +879,7 @@
     output_bgrad = jnp.sum(branch_grad.astype(f32), axis=0)
     attended_grad = jnp.einsum("re,de->rd", branch_grad, all_out, preferred_element_type=f32).astype(bf16)
     grad_mine = jnp.concatenate([mine(attended_grad), swap(others(attended_grad))], axis=0)
-    grad_heads = grad_mine.reshape(2 * rows, heads, HDIM)
-    delta = jnp.einsum("qhd,hqd->hq", grad_heads.astype(f32), exact)[..., None]
-    scores = jnp.einsum("qhd,khd->hqk", queries, keys, preferred_element_type=f32) * scaling
-    probs = jnp.exp(scores - log_total)
-    prob_grad = jnp.einsum("qhd,khd->hqk", grad_heads, values, preferred_element_type=f32)
-    score_grad = (probs * (prob_grad - delta)).astype(bf16)
-    probs_low = probs.astype(bf16)
-    query_grad = jnp.einsum("hqk,khd->qhd", score_grad, keys, preferred_element_type=f32) * scaling
-    key_grad = jnp.einsum("hqk,qhd->khd", score_grad, queries, preferred_element_type=f32) * scaling
-    value_grad = jnp.einsum("hqk,qhd->khd", probs_low, grad_heads, preferred_element_type=f32)
-    qkv_grad = jnp.concatenate(
-        [v.astype(bf16).reshape(2 * rows, half) for v in (query_grad, key_grad, value_grad)], axis=1
-    )
+    qkv_grad = attend_back(qkv, attended_mine, inverse, grad_mine, weights, 224)
     qkv_wgrad = jnp.einsum("rd,re->de", normed_one, qkv_grad, preferred_element_type=f32).astype(bf16)
     qkv_bgrad = jnp.sum(qkv_grad.astype(f32), axis=0)
     nothing = jnp.zeros((half,), f32)

time: 709 us -> 584 us (0.82)
  matrix products: 301 us -> 125 us
  Pallas kernels: 271 us -> 367 us
  other arithmetic: 49.7 us -> 22.4 us
  local copies, waits for them, and re-layouts: 39.1 us -> 18.4 us
    dot_general x6 -> x0, matrix products: 174 us -> none  [the longest x1 46 us: fast_device(): jnp.einsum('qhd,khd->hqk', grad_heads, values, preferred_element_type=f32)]
    pallas_call x0 -> x2, Pallas kernels: none -> 96.8 us  [the longest x1 51.9 us: attend_back(): pl.pallas_call(functools.partial(attend_back_kernel, block_rows), out_sha...]
    reduce_sum x1 -> x0, other arithmetic: 26 us -> none  [fast_device(): total = jnp.sum(weights, axis=-1, keepdims=True)]
    split x4 -> x0, local copies, waits for them, and re-layouts: 12.7 us -> none  [fast_device(): jnp.split(qkv, 3, axis=1)]
  transfers between devices with their start and end apart: 3 -> 3, of which waited for: 2 -> 3; matrix products, arithmetic and copies ran while one was open for 5% -> 6% of each run, Pallas kernels for 0% -> 0%
where the time goes in v2:
time: 584 us; the launch traced here: 579 us
  Pallas kernels  367 us (63%)
  matrix products  125 us (21%)
  waiting for transfers between devices  43.4 us (7%)
  other arithmetic  22.4 us (4%)
  local copies, waits for them, and re-layouts  18.4 us (3%)
    pallas_call x1, Pallas kernels, scatter_all(): pl.pallas_call(functools.partial(rs_kernel, depth, n, chunks, lag), out_s...  144 us
    pallas_call x1, Pallas kernels, gather_all(): pl.pallas_call(functools.partial(ag_kernel, depth, n, chunks, ahead, lag)...  125 us
    pallas_call x1, Pallas kernels, attend_back(): pl.pallas_call(functools.partial(attend_back_kernel, block_rows), out_sha...  51.9 us
    pallas_call x1, Pallas kernels, attend(): pl.pallas_call(functools.partial(attend_kernel, block_rows), out_shape=[j...  44.9 us
    ppermute x3, waiting for transfers between devices, swap(): return lax.ppermute(value, 'ctx', [(0, 1), (1, 0)])  43.4 us
    dot_general x1, matrix products, fast_device(): jnp.einsum('rd,fd->rf', cot_rows, all_down, preferred_element_type=f32)  21.5 us
    dot_general x1, matrix products, fast_device(): jnp.einsum('rf,rd->fd', hidden, cot_rows, preferred_element_type=f32)  16.7 us
    dot_general x1, matrix products, fast_device(): jnp.dot(hidden, all_down, preferred_element_type=f32)  14.8 us
  transfers between devices with their start and end apart: 3, of which 3 were waited for; matrix products, arithmetic and copies ran while one was open for 6% of the time, Pallas kernels for 0%

profile of v2, /device:TPU:0, one launch (start us, length us, event | category | flops | bytes accessed | tf_op | source)
XLA Modules:
  0.0 579.3 jit_solution(16402994660601952324)
XLA Ops:
  3.3 1.3 maximum_maximum_fusion.refs_0_
  4.6 125.5 %weights_gather.1 = (bf16[256,128]{1,0:T(8,128)(2,1)}, bf16[1024,1536]{1,0:T(8,128)(2,1)}, bf16[1024,1024]{1,0:T(8,128)(2,1)}, bf16[1024,4096]{1,0:T(8,128)(2,1)...) custom-call(bf16[16,128]{1,0:T(8,128)(2,1)} %maximum_maximum_fusion.refs_0_, ...), custom_call_target="tpu_custom_call" | custom-call | tf_op jit(solution)/shard_map/weights_gather/pallas_call | solution.py:469
  131.3 2.1 convert_reduce_fusion.1
  134.5 9.2 %add_convert_fusion.qkv = bf16[1568,1536]{1,0:T(8,128)(2,1)} fusion(bf16[1024,1536]{1,0:T(8,128)(2,1)S(1)} %copy-done.35, f32[1536]{0:T(1024)S(1)} %pad_maximum_fusion.3, f32[1024]{0:T(1024)S(1)} %bitcast.119, f32[1024]{0:T(1024)S(1)} %bitcast.105, f32[1568]{0:T(1024)S(1)} %add_rsqrt_fusion, f32[1568]{0:T(1024)S(1)} %broadcast_multiply_fusion, ...), kind=kOutput, calls=%fused_computation.16 | convolution fusion | flops 4951769088 | bytes 11200768 | tf_op jit(solution)/shard_map/dot_general | solution.py:852
  143.8 44.9 %attend.1 = (bf16[1568,512]{1,0:T(8,128)(2,1)}, f32[1568,512]{1,0:T(8,128)}, bf16[8,1568,1568]{2,1,0:T(8,128)(2,1)}) custom-call(bf16[1568,1536]{1,0:T(8,128)(2,1)} %add_convert_fusion.qkv), custom_call_target="tpu_custom_call" | custom-call | tf_op jit(solution)/shard_map/attend/pallas_call | solution.py:675
  188.7 2.6 fusion.50
  195.1 17.1 %collective-permute-done = bf16[784,512]{1,0:T(8,128)(2,1)} collective-permute-done((bf16[784,512]{1,0:T(8,128)(2,1)}, bf16[784,512]{1,0:T(8,128)(2,1)}, u32[]{:S(2)}, u32[]{:S(2)}) %collective-permute-start) | collective-permute-done | bytes 802848 | tf_op jit(solution)/shard_map/ppermute | solution.py:801
  212.2 3.7 fusion.54
  216.4 10.3 %fusion.43 = f32[784,4096]{1,0:T(8,128)} fusion(bf16[1024,4096]{1,0:T(8,128)(2,1)S(1)} %bitcast.135, f32[784,1024]{1,0:T(8,128)S(1)} %get-tuple-element.85, f32[1024]{0:T(1024)S(1)} %bitcast.121, f32[1024]{0:T(1024)S(1)} %bitcast.109, f32[784]{0:T(1024)S(1)} %fusion.38, f32[784]{0:T(1024)S(1)} %broadcast_multiply_fusion.2), kind=kOutput, calls=%fused_computation.113 | convolution fusion | flops 6580682752 | bytes 24459392 | tf_op jit(solution)/shard_map/dot_general | solution.py:859
  226.7 16.7 %convolution_convert_fusion.1.refs_4_ = bf16[4096,1024]{1,0:T(8,128)(2,1)} fusion(bf16[1,784,1024]{2,1,0:T(8,128)(2,1)S(1)} %copy-done.7, f32[784,4096]{1,0:T(8,128)} %fusion.43, f32[4096]{0:T(1024)S(1)} %bitcast.113), kind=kOutput, calls=%fused_computation.22 | convolution fusion | flops 6612975616 | bytes 22855680 | tf_op jit(solution)/shard_map/rf,rd->fd/dot_general | solution.py:866
  243.4 21.5 %fusion.55 = (bf16[4096]{0:T(1024)(128)(2,1)S(1)}, bf16[784,4096]{1,0:T(8,128)(2,1)}) fusion(f32[784,4096]{1,0:T(8,128)} %fusion.43, f32[4096]{0:T(1024)S(1)} %bitcast.114, bf16[4096,1024]{1,0:T(8,128)(2,1)} %get-tuple-element.37, bf16[1,784,1024]{2,1,0:T(8,128)(2,1)S(1)} %copy-done.7), kind=kOutput, calls=%fused_computation.122 | convolution fusion | flops 6647312384 | bytes 29286400 | tf_op jit(solution)/shard_map/rd,fd->rf/dot_general | solution.py:868
  264.9 14.8 %fusion.26 = bf16[1,784,1024]{2,1,0:T(8,128)(2,1)} fusion(f32[784,1024]{1,0:T(8,128)S(1)} %get-tuple-element.85, f32[1024]{0:T(1024)S(1)} %bitcast.123, bf16[4096,1024]{1,0:T(8,128)(2,1)} %get-tuple-element.37, f32[784,4096]{1,0:T(8,128)} %fusion.43, f32[4096]{0:T(1024)S(1)} %bitcast.115), kind=kOutput, calls=%fused_computation.55 | convolution fusion | flops 6611189760 | bytes 26071040 | tf_op jit(solution)/shard_map/dot_general | solution.py:861
  279.8 10.4 %multiply_reduce_fusion = (bf16[1024]{0:T(1024)(128)(2,1)S(1)}, f32[784]{0:T(1024)S(1)}, bf16[1024]{0:T(1024)(128)(2,1)S(1)}, f32[784,1024]{1,0:T(8,128)S(1)}) fusion(f32[784,1024]{1,0:T(8,128)S(1)} %get-tuple-element.85, f32[784]{0:T(1024)S(1)} %fusion.38, f32[784]{0:T(1024)S(1)} %broadcast_multiply_fusion.2, f32[1024]{0:T(1024)S(1)} %bitcast.110, ...), kind=kOutput, calls=%fused_computation.45 | convolution fusion | flops 6583088128 | bytes 21251264 | tf_op jit(solution)/shard_map/rf,df->rd/dot_general | solution.py:873
  290.2 1.0 fusion.49
  291.8 1.0 copy-done.4
  292.9 1.9 convolution_convert_fusion.4
  294.8 1.1 constant_dynamic-slice_fusion.1
  296.4 12.2 %convolution_convert_fusion.refs_3_ = bf16[1024,4096]{1,0:T(8,128)(2,1)} fusion(bf16[784,4096]{1,0:T(8,128)(2,1)S(1)} %bitcast.137, f32[784,1024]{1,0:T(8,128)S(1)} %get-tuple-element.85, f32[1024]{0:T(1024)S(1)} %bitcast.122, f32[1024]{0:T(1024)S(1)} %bitcast.112, f32[784]{0:T(1024)S(1)} %fusion.38, f32[784]{0:T(1024)S(1)} %broadcast_multiply_fusion.2), kind=kOutput, calls=%fused_computation.21 | convolution fusion | flops 6584877056 | bytes 18036864 | tf_op jit(solution)/shard_map/rd,rf->df/dot_general | solution.py:871
  308.8 5.6 convolution_convert_fusion.3.refs_2_
  314.4 1.4 collective-permute-done.1
  315.8 2.4 pad_maximum_fusion.1.grads
  318.2 51.9 %attend_back.1 = bf16[1568,1536]{1,0:T(8,128)(2,1)} custom-call(bf16[1568,1536]{1,0:T(8,128)(2,1)} %add_convert_fusion.qkv, bf16[1568,512]{1,0:T(8,128)(2,1)} %get-tuple-element.34.attended, f32[1568,512]{1,0:T(8,128)} %get-tuple-element.38.inverse, bf16[1568,512]{1,0:T(8,128)(2,1)} %pad_maximum_fusion.1.grads, ...), custom_call_target="tpu_custom_call" | custom-call | tf_op jit(solution)/shard_map/attend_back/pallas_call | solution.py:760
  370.2 8.2 %fusion.56 = f32[1568,1024]{1,0:T(8,128)S(1)} fusion(bf16[1568,1536]{1,0:T(8,128)(2,1)} %attend_back.1, bf16[1024,1536]{1,0:T(8,128)(2,1)} %get-tuple-element.33), kind=kOutput, calls=%fused_computation.123 | convolution fusion | flops 4932501504 | bytes 14385152 | tf_op jit(solution)/shard_map/re,de->rd/dot_general | solution.py:888
  379.2 1.4 slice.133
  382.3 10.6 %convolution_convert_fusion.2.refs_1_ = bf16[1024,1536]{1,0:T(8,128)(2,1)} fusion(bf16[1568,1536]{1,0:T(8,128)(2,1)} %attend_back.1, f32[1024]{0:T(1024)S(1)} %bitcast.120, f32[1024]{0:T(1024)S(1)} %bitcast.106, f32[1568]{0:T(1024)S(1)} %copy-done.29, f32[1568]{0:T(1024)S(1)} %copy-done.26, bf16[784,1024]{1,0:T(8,128)(2,1)} %get-tuple-element.31, ...), kind=kOutput, calls=%fused_computation.36 | convolution fusion | flops 4948525056 | bytes 11194624 | tf_op jit(solution)/shard_map/rd,re->de/dot_general | solution.py:883
  392.9 25.0 %collective-permute-done.2 = bf16[784,1024]{1,0:T(8,128)(2,1)} collective-permute-done((bf16[784,1024]{1,0:T(8,128)(2,1)}, bf16[784,1024]{1,0:T(8,128)(2,1)}, u32[]{:S(2)}, u32[]{:S(2)}) %collective-permute-start.2) | collective-permute-done | bytes 1605664 | tf_op jit(solution)/shard_map/ppermute | solution.py:801
  417.9 2.9 fusion.23
  421.8 144.5 %gradients_scatter.1 = (f32[16,128]{1,0:T(8,128)}, f32[64,3072]{1,0:T(8,128)}, f32[64,1024]{1,0:T(8,128)}, f32[64,4096]{1,0:T(8,128)}, f32[256,1024]{1,0:T(8,128)}) custom-call(bf16[256,128]{1,0:T(8,128)(2,1)} %bitcast.101, bf16[1024,1536]{1,0:T(8,128)(2,1)} %convolution_convert_fusion.2.refs_1_, bf16[1024,1024]{1,0:T(8,128)(2,1)} %convolution_convert_fusion.3.refs_2_, ...), custom_call_target="tpu_custom_call" | custom-call | tf_op jit(solution)/shard_map/gradients_scatter/pallas_call | solution.py:602
  566.3 1.5 slice_bitcast_fusion.1
  567.8 1.2 slice_bitcast_fusion
  569.1 3.8 fusion.48
  573.8 2.4 add_bitcast_fusion
  (144 shorter events, 17.4 us)
Async XLA Ops:
  0.7 130.7 %copy-start.2 = (bf16[1,784,1024]{2,1,0:T(8,128)(2,1)S(1)}, bf16[1,784,1024]{2,1,0:T(8,128)(2,1)}, u32[]{:S(2)}) copy-start(bf16[1,784,1024]{2,1,0:T(8,128)(2,1)} %param.17) | copy-start | bytes 4816900
  1.7 131.7 %copy-start.32 = (bf16[16]{0:T(256)(128)(2,1)}, bf16[16]{0:T(256)(128)(2,1)S(1)}, u32[]{:S(2)}) copy-start(bf16[16]{0:T(256)(128)(2,1)S(1)} %pad.26.clone) | copy-start | bytes 100
  133.4 10.3 %copy-start.25 = (f32[1568]{0:T(1024)}, f32[1568]{0:T(1024)S(1)}, u32[]{:S(2)}) copy-start(f32[1568]{0:T(1024)S(1)} %broadcast_multiply_fusion) | copy-start | bytes 18820
  134.5 9.3 %copy-start.28 = (f32[1568]{0:T(1024)}, f32[1568]{0:T(1024)S(1)}, u32[]{:S(2)}) copy-start(f32[1568]{0:T(1024)S(1)} %add_rsqrt_fusion) | copy-start | bytes 18820
  143.8 48.8 %copy-start.7 = (bf16[1,784,1024]{2,1,0:T(8,128)(2,1)S(1)}, bf16[1,784,1024]{2,1,0:T(8,128)(2,1)}, u32[]{:S(2)}) copy-start(bf16[1,784,1024]{2,1,0:T(8,128)(2,1)} %param.18) | copy-start | bytes 4816900
  191.3 20.8 %collective-permute-start = (bf16[784,512]{1,0:T(8,128)(2,1)}, bf16[784,512]{1,0:T(8,128)(2,1)}, u32[]{:S(2)}, u32[]{:S(2)}) collective-permute-start(bf16[784,512]{1,0:T(8,128)(2,1)} %get-tuple-element.60), channel_id=1, source_target_pairs={{0,1},{1,0},{2,3},{3,2},{4,5},{5,4},{6,7},{7,6},{8,9},{9,8},{10,11... | collective-permute-start | bytes 2408456 | tf_op jit(solution)/shard_map/ppermute | solution.py:801
  193.5 18.6 %copy-start.14 = (bf16[784,512]{1,0:T(8,128)(2,1)S(1)}, bf16[784,512]{1,0:T(8,128)(2,1)}, u32[]{:S(2)}) copy-start(bf16[784,512]{1,0:T(8,128)(2,1)} %get-tuple-element.59) | copy-start | bytes 2408452
  193.5 18.6 %copy-start.36 = (bf16[1024,1024]{1,0:T(8,128)(2,1)S(1)}, bf16[1024,1024]{1,0:T(8,128)(2,1)}, u32[]{:S(2)}) copy-start(bf16[1024,1024]{1,0:T(8,128)(2,1)} %get-tuple-element.35) | copy-start | bytes 6291460
  193.8 22.0 %copy-start.18 = (f32[784]{0:T(1024)}, f32[784]{0:T(1024)S(1)}, u32[]{:S(2)}) copy-start(f32[784]{0:T(1024)S(1)} %broadcast_multiply_fusion.1) | copy-start | bytes 9412
  194.4 21.4 %copy-start.20 = (f32[784]{0:T(1024)}, f32[784]{0:T(1024)S(1)}, u32[]{:S(2)}) copy-start(f32[784]{0:T(1024)S(1)} %fusion.20) | copy-start | bytes 9412
  212.1 4.2 slice-start
  212.2 4.2 slice-start.1
  291.2 5.1 slice-start.2
  295.8 13.0 %copy-start.15 = (bf16[784,512]{1,0:T(8,128)(2,1)S(1)}, bf16[784,512]{1,0:T(8,128)(2,1)}, u32[]{:S(2)}) copy-start(bf16[784,512]{1,0:T(8,128)(2,1)} %get-tuple-element.59) | copy-start | bytes 2408452
  295.8 20.0 %collective-permute-start.1 = (bf16[784,512]{1,0:T(8,128)(2,1)}, bf16[784,512]{1,0:T(8,128)(2,1)}, u32[]{:S(2)}, u32[]{:S(2)}) collective-permute-start(bf16[784,512]{1,0:T(8,128)(2,1)} %get-tuple-element.58), channel_id=1, source_target_pairs={{0,1},{1,0},{2,3},{3,2},{4,5},{5,4},{6,7},{7,6},{8,9},{9,8},{10,11... | collective-permute-start | bytes 2408456 | tf_op jit(solution)/shard_map/ppermute | solution.py:801
  370.2 8.2 %copy-start.6 = (bf16[1568,1536]{1,0:T(8,128)(2,1)S(1)}, bf16[1568,1536]{1,0:T(8,128)(2,1)}, u32[]{:S(2)}) copy-start(bf16[1568,1536]{1,0:T(8,128)(2,1)} %attend_back.1) | copy-start | bytes 14450692
  378.3 3.7 copy-start.34
  378.4 3.9 copy-start.3
  378.4 3.9 copy-start.23
  378.4 3.9 copy-start.26
  378.4 3.9 copy-start.29
  378.4 3.9 copy-start.31
  381.6 36.3 %collective-permute-start.2 = (bf16[784,1024]{1,0:T(8,128)(2,1)}, bf16[784,1024]{1,0:T(8,128)(2,1)}, u32[]{:S(2)}, u32[]{:S(2)}) collective-permute-start(bf16[784,1024]{1,0:T(8,128)(2,1)} %slice.133), channel_id=1, source_target_pairs={{0,1},{1,0},{2,3},{3,2},{4,5},{5,4},{6,7},{7,6},{8,9},{9,8},{10,11... | collective-permute-start | bytes 4816904 | tf_op jit(solution)/shard_map/ppermute | solution.py:801
  382.3 35.6 %copy-start.9 = (f32[1568,1024]{1,0:T(8,128)S(1)}, f32[1568,1024]{1,0:T(8,128)}, u32[]{:S(2)}) copy-start(f32[1568,1024]{1,0:T(8,128)} %copy-done.8) | copy-start | bytes 19267588
  382.3 35.6 %copy-start.19 = (f32[784]{0:T(1024)S(1)}, f32[784]{0:T(1024)}, u32[]{:S(2)}) copy-start(f32[784]{0:T(1024)} %copy-done.18) | copy-start | bytes 9412
  382.3 35.6 %copy-start.24 = (f32[784]{0:T(1024)S(1)}, f32[784]{0:T(1024)}, u32[]{:S(2)}) copy-start(f32[784]{0:T(1024)} %fusion.39) | copy-start | bytes 9412
  392.9 28.1 %copy-start.27 = (bf16[1,16,64]{2,1,0:T(8,128)(2,1)S(1)}, bf16[1,16,64]{2,1,0:T(8,128)(2,1)}, u32[]{:S(2)}) copy-start(bf16[1,16,64]{2,1,0:T(8,128)(2,1)} %stack.70) | copy-start | bytes 6148
  392.9 28.1 %copy-start.33 = (bf16[16]{0:T(256)(128)(2,1)S(1)}, bf16[16]{0:T(256)(128)(2,1)}, u32[]{:S(2)}) copy-start(bf16[16]{0:T(256)(128)(2,1)} %copy-done.32) | copy-start | bytes 100
  421.8 147.3 %copy-start.21 = (f32[784]{0:T(1024)S(1)}, f32[784]{0:T(1024)}, u32[]{:S(2)}) copy-start(f32[784]{0:T(1024)} %copy-done.20) | copy-start | bytes 9412
  569.1 3.8 copy-start.16
  569.1 4.7 copy-start.5
  573.8 5.0 copy-start.1
  (12 other events, 31.7 us)

commit v3 on v2

--- a/solution.py
+++ b/solution.py
@@ -352,17 +352,17 @@
         self.zs, self.zr, self.xs, self.xr, self.ys, self.yr, self.cs, self.cr, self.loc = sems
         self.where = where
     def src(self, ch, half):
-        t, r0, h, both = self.chunks[ch]
-        if not both: return self.ins[t].at[pl.ds(r0, h)]
+        t, r0, h, c0, w, both = self.chunks[ch]
+        if not both: return self.ins[t].at[pl.ds(r0, h), pl.ds(c0, w)]
         h2 = h // 2
-        return self.ins[t].at[pl.ds(pl.multiple_of(r0 + half * h2, 16), h2)]
+        return self.ins[t].at[pl.ds(pl.multiple_of(r0 + half * h2, 16), h2), pl.ds(c0, w)]
     def dst(self, ch, dz, dx, dc, half):
-        t, r0, h, both = self.chunks[ch]
+        t, r0, h, c0, w, both = self.chunks[ch]
         full = self.ins[t].shape[0]
         start = (dz * 4 + dx * 2 + dc) * full + r0
-        if not both: return self.outs[t].at[pl.ds(pl.multiple_of(start, 16), h)]
+        if not both: return self.outs[t].at[pl.ds(pl.multiple_of(start, 16), h), pl.ds(c0, w)]
         h2 = h // 2
-        return self.outs[t].at[pl.ds(pl.multiple_of(start + half * h2, 16), h2)]
+        return self.outs[t].at[pl.ds(pl.multiple_of(start + half * h2, 16), h2), pl.ds(c0, w)]
     def copy(self, src, dst, s, r, dz, dx, dc, dy):
         return pltpu.make_async_remote_copy(src_ref=src, dst_ref=dst, send_sem=s, recv_sem=r,
             device_id=(dz * 4 + dx * 2 + dc, dy), device_id_type=MESH)
@@ -393,29 +393,29 @@
         return self.copy(s, d, self.cs.at[ch, n], self.cr.at[ch, n], z, x, 1 - c, y)
     def own(self, ch):
         z, x, c, y = self.where
-        t, r0, h, both = self.chunks[ch]
+        t, r0, h, c0, w, both = self.chunks[ch]
         full = self.ins[t].shape[0]
-        return pltpu.make_async_copy(self.ins[t].at[pl.ds(r0, h)],
-            self.outs[t].at[pl.ds(pl.multiple_of((z * 4 + x * 2 + c) * full + r0, 16), h)], self.loc.at[ch])
+        return pltpu.make_async_copy(self.ins[t].at[pl.ds(r0, h), pl.ds(c0, w)],
+            self.outs[t].at[pl.ds(pl.multiple_of((z * 4 + x * 2 + c) * full + r0, 16), h), pl.ds(c0, w)], self.loc.at[ch])
     def begin(self, ch):
         for k in range(1, self.depth): self.zmove(ch, k).start()
         self.xmove(ch, 0).start()
         self.cmove(ch, 0, 0, False).start()
-        if self.chunks[ch][3]: self.cmove(ch, 0, 0, True).start()
+        if self.chunks[ch][5]: self.cmove(ch, 0, 0, True).start()
         self.own(ch).start()
     def zstage(self, ch):
         for k in range(1, self.depth):
             self.zmove(ch, k, True).wait_recv()
             self.xmove(ch, k).start()
-            if self.chunks[ch][3]: self.ymove(ch, 0, k).start()
+            if self.chunks[ch][5]: self.ymove(ch, 0, k).start()
             self.cmove(ch, 0, k, False).start()
     def xstage(self, ch):
         for j in range(self.depth):
             self.xmove(ch, j, True).wait_recv()
-            if self.chunks[ch][3]: self.ymove(ch, 1, j).start()
+            if self.chunks[ch][5]: self.ymove(ch, 1, j).start()
             self.cmove(ch, 1, j, False).start()
     def ystage(self, ch):
-        if not self.chunks[ch][3]: return
+        if not self.chunks[ch][5]: return
         for i in range(2):
             for j in range(1 - i, self.depth):
                 self.ymove(ch, i, j, True).wait_recv()
@@ -424,10 +424,10 @@
         for i in range(2):
             for j in range(self.depth):
                 self.cmove(ch, i, j, False, True).wait_recv()
-                if self.chunks[ch][3]: self.cmove(ch, i, j, True, True).wait_recv()
+                if self.chunks[ch][5]: self.cmove(ch, i, j, True, True).wait_recv()
         self.own(ch).wait()
     def sent(self, ch):
-        both = self.chunks[ch][3]
+        both = self.chunks[ch][5]
         for k in range(1, self.depth): self.zmove(ch, k).wait_send()
         for j in range(self.depth): self.xmove(ch, j).wait_send()
         for i in range(2):
@@ -440,41 +440,6 @@
 def gather_sems(depth, n):
     S = pltpu.SemaphoreType.DMA
     return [S((n, depth)), S((n, depth)), S((n, depth)), S((n, depth)), S((n, 2 * depth)), S((n, 2 * depth)), S((n, 4 * depth)), S((n, 4 * depth)), S((n,))]
-
-def ag_kernel(depth, n, chunks, ahead, lag, *refs):
-    ins = refs[:n]; x_in = refs[n]
-    outs = refs[n + 1:2 * n + 1]; x_out = refs[2 * n + 1]
-    sems = refs[2 * n + 2:2 * n + 11]; ys, yr = refs[2 * n + 11:]
-    z, x, c, y = place()
-    g = Gather(depth, chunks, ins, outs, sems, (z, x, c, y))
-    greet(z, x, c, y, depth)
-    xw = g.copy(x_in, x_out, ys, yr, z, x, c, 1 - y)
-    xw.start()
-    N = len(chunks)
-    for ch in range(min(ahead, N)): g.begin(ch)
-    for s in range(N + 2 * lag):
-        if s < N:
-            g.zstage(s)
-            if s + ahead < N: g.begin(s + ahead)
-        if 0 <= s - lag < N: g.xstage(s - lag)
-        if 0 <= s - 2 * lag < N: g.ystage(s - 2 * lag)
-    xw.wait()
-    for ch in range(N): g.arrived(ch)
-    for ch in range(N): g.sent(ch)
-
-
-def gather_all(shards, x, chunks, depth=4, ahead=2, lag=1, cid=1):
-    n = len(shards)
-    S = pltpu.SemaphoreType.DMA
-    return pl.pallas_call(
-        functools.partial(ag_kernel, depth, n, chunks, ahead, lag),
-        out_shape=[jax.ShapeDtypeStruct((depth * 4 * s.shape[0],) + s.shape[1:], s.dtype) for s in shards] + [jax.ShapeDtypeStruct(x.shape, x.dtype)],
-        in_specs=[pl.BlockSpec(memory_space=pl.ANY)] * (n + 1),
-        out_specs=[pl.BlockSpec(memory_space=pl.ANY)] * (n + 1),
-        scratch_shapes=gather_sems(depth, len(chunks)) + [S, S],
-        compiler_params=pltpu.CompilerParams(collective_id=cid, has_side_effects=True),
-        name="weights_gather")(*shards, x)
-
 
 def rowwise(h, w, body):
     wide = min(w, 1024 if w % 1024 == 0 else 512)
@@ -609,86 +574,397 @@
         name="gradients_scatter")(*grads)
 
 
+DEPTH, BOTH = 4, 2
+f32, bf16 = jnp.float32, jnp.bfloat16
 NT = (((1,), (1,)), ((), ()))
 NN = (((1,), (0,)), ((), ()))
-
-
-def attend_kernel(block_rows, qkv, attended, inverse, weights_out, values_ones, kept, sem):
-    length = qkv.shape[0]
-    half = qkv.shape[1] // 3
-    blocks, pairs = length // block_rows, half // 128
-    low_lanes = lax.broadcasted_iota(jnp.int32, (block_rows, 128), 1) < HDIM
-
-    def out(pair, block, head, slot):
-        rows = pl.ds(pl.multiple_of(block * block_rows, 16), block_rows)
-        return pltpu.make_async_copy(kept.at[slot, head], weights_out.at[2 * pair + head, rows], sem.at[slot, head])
-
-    values_ones[:, 128:] = jnp.ones((length, 128), jnp.bfloat16)
-
-    def one_pair(pair, _):
-        at = pl.multiple_of(pair * 128, 128)
-        values_ones[:, :128] = qkv[:, pl.ds(2 * half + at, 128)]
-
-        def one_block(block, _):
-            turn = pair * blocks + block
+TN = (((0,), (0,)), ((), ()))
+SQRT_2_PI = 0.7978845608028654
+
+
+def mul(a, b, dims):
+    return lax.dot_general(a, b, dims, preferred_element_type=f32)
+
+
+def tall(i, size):
+    return pl.ds(pl.multiple_of(i * size, 16), size)
+
+
+def normalized(rows):
+    centered = rows - jnp.mean(rows, axis=-1, keepdims=True)
+    inverse = lax.rsqrt(jnp.mean(centered * centered, axis=-1, keepdims=True) + epsilon)
+    return centered * inverse, inverse
+
+
+GAIN_ONE, SHIFT_ONE, QUERY_BIAS, VALUE_BIAS, OUTPUT_BIAS, GAIN_TWO, SHIFT_TWO, DOWN_BIAS = range(8)
+
+
+def forward_kernel(depth, chunks, ahead, *refs):
+    (
+        small, own_qkv, own_out, own_up, own_down, x_own, cot,
+        all_small, all_qkv, all_out, all_up, all_down,
+        normed_out, qkv_out, exact_out, inverse_out, weights_out,
+        block_out, mid_grad_out, attended_grad_out, out_wgrad, up_wgrad, down_wgrad, vec_grads, up_bgrad,
+        x_other, attended, vecs, up_bias, mid, normed_two,
+    ) = refs[:31]
+    sems = refs[31:40]
+    swap_s, swap_r, att_s, att_r, loc, keep_sem = refs[40:]
+    z, x, c, y = place()
+    rows, width = x_own.shape
+    length, half = BOTH * rows, width // BOTH
+    pairs = half // 128
+    wide = up_bias.shape[1]
+    step = 112
+    g = Gather(depth, chunks, (small, own_qkv, own_out, own_up, own_down), (all_small, all_qkv, all_out, all_up, all_down), sems, (z, x, c, y))
+    greet(z, x, c, y, depth)
+    total = len(chunks)
+    swapping = g.copy(x_own, x_other, swap_s, swap_r, z, x, c, 1 - y)
+
+    def service(s):
+        if s < total:
+            g.zstage(s)
+            if s + ahead < total:
+                g.begin(s + ahead)
+        if 0 <= s - 1 < total:
+            g.xstage(s - 1)
+        if 0 <= s - 2 < total:
+            g.ystage(s - 2)
+
+    for ch in range(ahead):
+        g.begin(ch)
+        if ch == 1:
+            swapping.start()
+    service(0)
+    service(1)
+    g.arrived(0)
+
+    def first_phase(small_v, normed, qkv, exact, inverse, weight, values_ones, kept):
+        get = pltpu.make_async_copy(all_small, small_v, loc.at[0])
+        get.start()
+        get.wait()
+        for chip in range(2 * depth):
+            one, two = small_v[pl.ds(32 * chip, 16), :].astype(f32), small_v[pl.ds(32 * chip + 16, 16), :].astype(f32)
+            vecs[0:8, 128 * chip : 128 * chip + 128] = one[0:8] + two[0:8]
+            for core, part in enumerate((one, two)):
+                for n in range(2):
+                    at = (2 * chip + core) * 256 + 128 * n
+                    up_bias[0:1, at : at + 128] = part[8 + n : 9 + n]
+
+        def norm_one(source, first):
+            gain, shift = vecs[GAIN_ONE : GAIN_ONE + 1, :], vecs[SHIFT_ONE : SHIFT_ONE + 1, :]
+
+            def one(i, _):
+                value = normalized(source[tall(i, step), :].astype(f32))[0]
+                normed[pl.ds(pl.multiple_of(first + i * step, 16), step), :] = (value * gain + shift).astype(bf16)
+                return 0
+
+            lax.fori_loop(0, rows // step, one, 0)
+
+        mine = pl.ds(pl.multiple_of(y * half, 128), half)
+
+        def project(first):
+            these = pl.ds(first, rows)
+            for n, bias in enumerate((QUERY_BIAS, None, VALUE_BIAS)):
+                value = mul(normed[these, :], weight[:, n * half : (n + 1) * half], NN)
+                if bias is not None:
+                    value = value + vecs[bias : bias + 1, mine]
+                qkv[these, n * half : (n + 1) * half] = value.astype(bf16)
+
+        norm_one(x_own, 0)
+        service(2)
+        g.arrived(1)
+        get = pltpu.make_async_copy(all_qkv, weight, loc.at[0])
+        get.start()
+        get.wait()
+        project(0)
+        swapping.wait_recv()
+        norm_one(x_other, rows)
+        project(rows)
+        put_normed = pltpu.make_async_copy(normed, normed_out, loc.at[1])
+        put_qkv = pltpu.make_async_copy(qkv, qkv_out, loc.at[2])
+        put_normed.start()
+        put_qkv.start()
+        service(3)
+
+        low_lanes = lax.broadcasted_iota(jnp.int32, (rows, 128), 1) < HDIM
+
+        def keep(pair, block, head, slot):
+            return pltpu.make_async_copy(kept.at[slot, head], weights_out.at[2 * pair + head, tall(block, rows)], keep_sem.at[slot, head])
+
+        def send(pair):
+            at = pl.multiple_of(pair * 128, 128)
+            there = pl.multiple_of(y * half + at, 128)
+            return g.copy(
+                exact_low.at[:, pl.ds(at, 128)], attended.at[:, pl.ds(there, 128)], att_s.at[pair], att_r.at[pair], z, x, c, 1 - y
+            )
+
+        exact_low = normed_two
+        values_ones[:, 128:] = jnp.ones((length, 128), bf16)
+
+        def attend(turn, _):
+            pair = turn // 2
             slot = turn % 2
+            block = 1 - slot
+            for n, s in ((1, 4), (4, 5), (6, 6), (7, 7)):
+
+                @pl.when(turn == n)
+                def _(s=s):
+                    service(s)
 
             @pl.when(turn > 1)
             def _():
                 for head in range(2):
-                    out(0, 0, head, slot).wait()
-
-            rows = pl.ds(pl.multiple_of(block * block_rows, 16), block_rows)
-            queries = qkv[rows, pl.ds(at, 128)] * jnp.bfloat16(HDIM**-0.5)
+                    keep(0, 0, head, slot).wait()
+
+            at = pl.multiple_of(pair * 128, 128)
+
+            @pl.when(slot == 0)
+            def _():
+                values_ones[:, :128] = qkv[:, pl.ds(2 * half + at, 128)]
+
+            these = tall(block, rows)
+            queries = qkv[these, pl.ds(at, 128)] * bf16(HDIM**-0.5)
             keys = qkv[:, pl.ds(half + at, 128)]
             values = values_ones[...]
             parts = []
             for head in range(2):
                 masked = jnp.where(low_lanes == (head == 0), queries, jnp.zeros_like(queries))
-                scores = lax.dot_general(masked, keys, NT, preferred_element_type=jnp.float32)
+                scores = mul(masked, keys, NT)
                 top = jnp.max(scores, axis=1, keepdims=True)
-                weights = jnp.exp(scores - top).astype(jnp.bfloat16)
+                weights = jnp.exp(scores - top).astype(bf16)
                 kept[slot, head] = weights
-                summed = lax.dot_general(weights, values, NN, preferred_element_type=jnp.float32)
+                summed = mul(weights, values, NN)
                 parts.append((summed[:, :128], 1.0 / summed[:, 128:]))
             (low, low_inverse), (high, high_inverse) = parts
             scale = jnp.where(low_lanes, low_inverse, high_inverse)
-            attended[rows, pl.ds(at, 128)] = (jnp.where(low_lanes, low, high) * scale).astype(jnp.bfloat16)
-            inverse[rows, pl.ds(at, 128)] = scale
+            value = jnp.where(low_lanes, low, high) * scale
+            exact[these, pl.ds(at, 128)] = value
+            inverse[these, pl.ds(at, 128)] = scale
             for head in range(2):
-                out(pair, block, head, slot).start()
+                keep(pair, block, head, slot).start()
+
+            @pl.when(slot == 0)
+            def _():
+                exact_low[:, pl.ds(at, 128)] = value.astype(bf16)
+                send(pair).start()
+
+            @pl.when(slot == 1)
+            def _():
+                attended[:, pl.ds(pl.multiple_of(y * half + at, 128), 128)] = value.astype(bf16)
+
             return 0
 
-        lax.fori_loop(0, blocks, one_block, 0)
-        return 0
-
-    lax.fori_loop(0, pairs, one_pair, 0)
-    for slot in range(2):
-        for head in range(2):
-            out(0, 0, head, slot).wait()
-
-
-def attend(qkv, block_rows):
-    length, wide = qkv.shape
-    half = wide // 3
-    whole = pl.BlockSpec(memory_space=pltpu.VMEM)
+        lax.fori_loop(0, 2 * pairs, attend, 0)
+        put_exact = pltpu.make_async_copy(exact, exact_out, loc.at[3])
+        put_inverse = pltpu.make_async_copy(inverse, inverse_out, loc.at[4])
+        put_exact.start()
+        put_inverse.start()
+        for slot in range(2):
+            for head in range(2):
+                keep(0, 0, head, slot).wait()
+        for pair in range(pairs):
+            send(pair).wait()
+        for put in (put_normed, put_qkv, put_exact, put_inverse):
+            put.wait()
+
+    V = pltpu.VMEM
+    pl.run_scoped(
+        first_phase,
+        V(all_small.shape, bf16),
+        V((length, width), bf16),
+        V((length, 3 * half), bf16),
+        V((length, half), f32),
+        V((length, half), f32),
+        V((width, 3 * half), bf16),
+        V((length, 256), bf16),
+        V((2, 2, rows, length), bf16),
+    )
+
+    def second_phase(out_w, up_w, down_w, low_t, block_sum, normed_grad, up_stage, down_stage):
+        tiles = wide // width
+
+        def get_down(j, slot):
+            return pltpu.make_async_copy(all_down.at[pl.ds(pl.multiple_of(j * width, 16), width)], down_w.at[slot], loc.at[1 + slot])
+
+        def get_up(j):
+            return pltpu.make_async_copy(all_up.at[:, pl.ds(pl.multiple_of(j * width, 128), width)], up_w, loc.at[3])
+
+        def put_up(j):
+            return pltpu.make_async_copy(up_stage, up_wgrad.at[:, pl.ds(pl.multiple_of(j * width, 128), width)], loc.at[4])
+
+        def put_down(j):
+            return pltpu.make_async_copy(down_stage, down_wgrad.at[pl.ds(pl.multiple_of(j * width, 16), width)], loc.at[5])
+
+        g.arrived(6)
+        get = pltpu.make_async_copy(all_out, out_w, loc.at[0])
+        get.start()
+        for ch in range(2, 6):
+            g.arrived(ch)
+        get_down(0, 0).start()
+        get.wait()
+        mid[...] = mul(attended[...], out_w[...], NN)
+
+        def norm_two(i, _):
+            these = tall(i, step)
+            value = mid[these, :] + vecs[OUTPUT_BIAS : OUTPUT_BIAS + 1, :] + x_own[these, :].astype(f32)
+            mid[these, :] = value
+            value = normalized(value)[0] * vecs[GAIN_TWO : GAIN_TWO + 1, :] + vecs[SHIFT_TWO : SHIFT_TWO + 1, :]
+            normed_two[these, :] = value.astype(bf16)
+            return 0
+
+        lax.fori_loop(0, rows // step, norm_two, 0)
+        low_t[...] = normed_two[...].T
+        block_sum[...] = jnp.zeros_like(block_sum)
+        normed_grad[...] = jnp.zeros_like(normed_grad)
+
+        def feed(j, _):
+            slot = j % 2
+            for n in range(tiles):
+
+                @pl.when(j == n)
+                def _(n=n):
+                    service(8 + n)
+                    g.arrived(7 + n)
+
+            get_up(j).start()
+            get_down(j, slot).wait()
+
+            @pl.when(j + 1 < tiles)
+            def _():
+                get_down(j + 1, 1 - slot).start()
+
+            @pl.when(j > 0)
+            def _():
+                put_up(0).wait()
+                put_down(0).wait()
+
+            get_up(j).wait()
+            cols = pl.ds(pl.multiple_of(j * width, 128), width)
+            up, down = up_w[...], down_w[slot]
+            u = mul(normed_two[...], up, NN) + up_bias[0:1, cols]
+            hidden_grad = mul(cot[...], down, NT)
+            inner = jnp.tanh(SQRT_2_PI * (u + 0.044715 * (u * u * u)))
+            hidden = (0.5 * u * (1.0 + inner)).astype(bf16)
+            slope = 0.5 * (1.0 + inner) + 0.5 * u * (1.0 - inner * inner) * (SQRT_2_PI * (1.0 + 3 * 0.044715 * (u * u)))
+            grad = hidden_grad * slope
+            pre_grad = grad.astype(bf16)
+            block_sum[...] += mul(hidden, down, NN)
+            down_stage[...] = mul(hidden, cot[...], TN).astype(bf16)
+            up_stage[...] = mul(low_t[...], pre_grad, NN).astype(bf16)
+            up_bgrad[0:1, cols] = jnp.sum(pre_grad.astype(f32), axis=0, keepdims=True)
+            normed_grad[...] += mul(pre_grad, up, NT)
+            put_up(j).start()
+            put_down(j).start()
+            return 0
+
+        lax.fori_loop(0, tiles, feed, 0)
+
+        zero = jnp.zeros((1, width), f32)
+
+        def back_two(i, sums):
+            gain_sum, shift_sum, out_sum, cot_sum = sums
+            these = tall(i, step)
+            rows_in = mid[these, :]
+            block_sum[these, :] = block_sum[these, :] + rows_in + vecs[DOWN_BIAS : DOWN_BIAS + 1, :]
+            zed, inverse = normalized(rows_in)
+            grad = normed_grad[these, :]
+            scaled = grad * vecs[GAIN_TWO : GAIN_TWO + 1, :]
+            part = inverse * (
+                scaled - jnp.mean(scaled, axis=-1, keepdims=True) - zed * jnp.mean(scaled * zed, axis=-1, keepdims=True)
+            )
+            above = cot[these, :].astype(f32)
+            whole = above + part
+            mid[these, :] = whole
+            branch = whole.astype(bf16)
+            normed_two[these, :] = branch
+            add = lambda total, value: total + jnp.sum(value, axis=0, keepdims=True)
+            return (
+                add(gain_sum, grad * zed), add(shift_sum, grad), add(out_sum, branch.astype(f32)), add(cot_sum, above),
+            )
+
+        gain_sum, shift_sum, out_sum, cot_sum = lax.fori_loop(0, rows // step, back_two, (zero,) * 4)
+        vec_grads[...] = jnp.zeros_like(vec_grads)
+        vec_grads[GAIN_TWO : GAIN_TWO + 1, :] = gain_sum
+        vec_grads[SHIFT_TWO : SHIFT_TWO + 1, :] = shift_sum
+        vec_grads[OUTPUT_BIAS : OUTPUT_BIAS + 1, :] = out_sum
+        vec_grads[DOWN_BIAS : DOWN_BIAS + 1, :] = cot_sum
+        put_mid = pltpu.make_async_copy(mid, mid_grad_out, loc.at[0])
+        put_mid.start()
+        put_up(0).wait()
+        put_down(0).wait()
+        block_out[...] = block_sum[...].astype(bf16)
+        up_stage[...] = mul(attended[...], normed_two[...], TN).astype(bf16)
+        put_out = pltpu.make_async_copy(up_stage, out_wgrad, loc.at[4])
+        put_out.start()
+        attended_grad_out[...] = mul(normed_two[...], out_w[...], NT).astype(bf16)
+        put_mid.wait()
+        put_out.wait()
+
+    pl.run_scoped(
+        second_phase,
+        V((width, width), bf16),
+        V((width, width), bf16),
+        V((2, width, width), bf16),
+        V((width, rows), bf16),
+        V((rows, width), f32),
+        V((rows, width), f32),
+        V((width, width), bf16),
+        V((width, width), bf16),
+    )
+    swapping.wait_send()
+    for ch in range(total):
+        g.sent(ch)
+
+
+def forward(small, own_qkv, own_out, own_up, own_down, x_own, cot, depth=DEPTH, ahead=3):
+    rows, width = x_own.shape
+    length, half, wide = BOTH * rows, width // BOTH, own_up.shape[1]
+    chunks = gather_chunks(own_up.shape, own_down.shape)
+    S, V = pltpu.SemaphoreType.DMA, pltpu.VMEM
+    anywhere, fast = pl.BlockSpec(memory_space=pl.ANY), pl.BlockSpec(memory_space=pltpu.VMEM)
+    shape = jax.ShapeDtypeStruct
+    parts = 4 * depth
     return pl.pallas_call(
-        functools.partial(attend_kernel, block_rows),
-        out_shape=[
-            jax.ShapeDtypeStruct((length, half), jnp.bfloat16),
-            jax.ShapeDtypeStruct((length, half), jnp.float32),
-            jax.ShapeDtypeStruct((half // HDIM, length, length), jnp.bfloat16),
+        functools.partial(forward_kernel, depth, chunks, ahead),
+        out_shape=[shape((parts * s.shape[0], s.shape[1]), bf16) for s in (small, own_qkv, own_out, own_up, own_down)]
+        + [
+            shape((length, width), bf16),
+            shape((length, 3 * half), bf16),
+            shape((length, half), f32),
+            shape((length, half), f32),
+            shape((half // HDIM, length, length), bf16),
+            shape((rows, width), bf16),
+            shape((rows, width), f32),
+            shape((rows, width), bf16),
+            shape((width, width), bf16),
+            shape((width, wide), bf16),
+            shape((wide, width), bf16),
+            shape((8, width), f32),
+            shape((1, wide), f32),
         ],
-        in_specs=[whole],
-        out_specs=[whole, whole, pl.BlockSpec(memory_space=pl.ANY)],
+        in_specs=[anywhere] * 5 + [fast] * 2,
+        out_specs=[anywhere] * 10 + [fast, anywhere, fast] + [anywhere] * 3 + [fast] * 2,
         scratch_shapes=[
-            pltpu.VMEM((length, 256), jnp.bfloat16),
-            pltpu.VMEM((2, 2, block_rows, length), jnp.bfloat16),
-            pltpu.SemaphoreType.DMA((2, 2)),
-        ],
-        compiler_params=pltpu.CompilerParams(vmem_limit_bytes=60 * 2**20),
-        name="attend",
-    )(qkv)
+            V((rows, width), bf16), V((rows, width), bf16), V((8, width), f32), V((1, wide), f32),
+            V((rows, width), f32), V((rows, width), bf16),
+        ]
+        + gather_sems(depth, len(chunks))
+        + [S, S, S((half // 128,)), S((half // 128,)), S((6,)), S((2, 2))],
+        compiler_params=pltpu.CompilerParams(collective_id=1, has_side_effects=True, vmem_limit_bytes=62 * 2**20),
+        name="forward_and_feed",
+    )(small, own_qkv, own_out, own_up, own_down, x_own, cot)
+
+
+def gather_chunks(up_shape, down_shape):
+    tall_up, wide = up_shape
+    tall_down, width = down_shape
+    quarter = tall_down // 4
+    return (
+        (0, 0, 16, 0, 128, False),
+        (1, 0, tall_up, 0, 3 * width // BOTH, False),
+    ) + tuple((4, quarter * i, quarter, 0, width, True) for i in range(4)) + ((2, 0, tall_up, 0, width, False),) + tuple(
+        (3, 0, tall_up, width * i, width, False) for i in range(wide // width)
+    )
 
 
 def attend_back_kernel(block_rows, qkv, attended, inverse, grads, weights_in, out, key_sum, value_sum, kept, sem):
@@ -723,8 +999,8 @@
             keys = qkv[:, pl.ds(half + at, 128)]
             values = qkv[:, pl.ds(2 * half + at, 128)]
             scaled = grads[rows, pl.ds(at, 128)].astype(jnp.float32) * inverse[rows, pl.ds(at, 128)]
-            product = scaled * attended[rows, pl.ds(at, 128)].astype(jnp.float32)
             low = scaled.astype(jnp.bfloat16)
+            product = low.astype(jnp.float32) * attended[rows, pl.ds(at, 128)]
             queries_t, low_t = queries.T, low.T
             query_parts, key_parts, value_parts = [], [], []
             for head in range(2):
@@ -773,9 +1049,6 @@
     )(qkv, attended, inverse, grads, weights)
 
 
-DEPTH, BOTH = 4, 2
-
-
 def pack_small(vectors, up_bias, c):
     rows = jnp.stack(vectors)
     zero = jnp.zeros_like(rows)
@@ -799,15 +1072,6 @@
 
 def swap(value):
     return lax.ppermute(value, "ctx", [(0, 1), (1, 0)])
-
-
-def gather_chunks():
-    return (
-        (0, 0, 16, False),
-        (1, 0, 64, False),
-    ) + tuple((4, 64 * i, 64, True) for i in range(4)) + ((2, 0, 64, False),) + tuple(
-        (3, 16 * i, 16, False) for i in range(4)
-    )
 
 
 def scatter_chunks():
@@ -840,46 +1104,14 @@
     )
     own_qkv = jnp.concatenate([mine(query_weight), mine(key_weight), mine(value_weight)], axis=1)
     x_own = activations[0]
-    all_small, all_qkv, all_out, all_up, all_down, x_other = gather_all(
-        (small, own_qkv, output_weight, up_weight, down_weight), x_own, gather_chunks()
-    )
-    vectors, full_up_bias = unpack_small(all_small)
-    gain_one, shift_one, full_query_bias, full_value_bias, full_output_bias, gain_two, shift_two, full_down_bias = vectors
-
-    token_rows = jnp.concatenate([x_own, x_other], axis=0).astype(f32)
-    normed_one = layer_norm(token_rows, gain_one, shift_one).astype(bf16)
-    bias = jnp.concatenate([mine(full_query_bias), jnp.zeros((half,), f32), mine(full_value_bias)])
-    qkv = (jnp.dot(normed_one, all_qkv, preferred_element_type=f32) + bias).astype(bf16)
-    attended_mine, inverse, weights = attend(qkv, rows)
-    attended = both(attended_mine[:rows], swap(attended_mine[rows:]))
-
+    (
+        all_small, all_qkv, _, _, _, normed_one, qkv, exact, inverse, weights, block_out, mid_grad, attended_grad,
+        output_wgrad, up_wgrad, down_wgrad, vec_grads, up_bgrad,
+    ) = forward(small, own_qkv, output_weight, up_weight, down_weight, x_own, cotangent[0])
     x_rows = x_own.astype(f32)
-    mid_rows = x_rows + jnp.dot(attended, all_out, preferred_element_type=f32) + full_output_bias
-    normed_two = layer_norm(mid_rows, gain_two, shift_two).astype(bf16)
-    pre_act = jnp.dot(normed_two, all_up, preferred_element_type=f32) + full_up_bias
-    hidden = gelu_act(pre_act).astype(bf16)
-    block_rows = mid_rows + jnp.dot(hidden, all_down, preferred_element_type=f32) + full_down_bias
-    block_out = block_rows.astype(bf16).reshape(activations.shape)
-
-    cot_rows = cotangent[0]
-    outer_grad = cot_rows.astype(f32)
-    down_wgrad = jnp.einsum("rf,rd->fd", hidden, cot_rows, preferred_element_type=f32).astype(bf16)
-    down_bgrad = jnp.sum(outer_grad, axis=0)
-    hidden_grad = jnp.einsum("rd,fd->rf", cot_rows, all_down, preferred_element_type=f32)
-    _, gelu_back = jax.vjp(gelu_act, pre_act)
-    pre_grad = gelu_back(hidden_grad)[0].astype(bf16)
-    up_wgrad = jnp.einsum("rd,rf->df", normed_two, pre_grad, preferred_element_type=f32).astype(bf16)
-    up_bgrad = jnp.sum(pre_grad.astype(f32), axis=0)
-    normed_two_grad = jnp.einsum("rf,df->rd", pre_grad, all_up, preferred_element_type=f32)
-    _, norm_two_back = jax.vjp(layer_norm, mid_rows, gain_two, shift_two)
-    mid_part, gain_two_grad, shift_two_grad = norm_two_back(normed_two_grad)
-    mid_grad = outer_grad + mid_part
-    branch_grad = mid_grad.astype(bf16)
-    output_wgrad = jnp.einsum("rd,re->de", attended, branch_grad, preferred_element_type=f32).astype(bf16)
-    output_bgrad = jnp.sum(branch_grad.astype(f32), axis=0)
-    attended_grad = jnp.einsum("re,de->rd", branch_grad, all_out, preferred_element_type=f32).astype(bf16)
+    gain_one, shift_one = unpack_small(all_small)[0][:2]
     grad_mine = jnp.concatenate([mine(attended_grad), swap(others(attended_grad))], axis=0)
-    qkv_grad = attend_back(qkv, attended_mine, inverse, grad_mine, weights, 224)
+    qkv_grad = attend_back(qkv, exact, inverse, grad_mine, weights, 224)
     qkv_wgrad = jnp.einsum("rd,re->de", normed_one, qkv_grad, preferred_element_type=f32).astype(bf16)
     qkv_bgrad = jnp.sum(qkv_grad.astype(f32), axis=0)
     nothing = jnp.zeros((half,), f32)
@@ -891,14 +1123,14 @@
     input_part, gain_one_grad, shift_one_grad = norm_one_back(normed_one_grad)
     input_grad = (mid_grad + input_part).reshape(activations.shape)
     small_grads = pack_small_grads(
-        (gain_one_grad, shift_one_grad, query_bgrad, value_bgrad, output_bgrad, gain_two_grad, shift_two_grad, down_bgrad),
-        up_bgrad,
+        (gain_one_grad, shift_one_grad, query_bgrad, value_bgrad) + tuple(vec_grads[n] for n in range(OUTPUT_BIAS, DOWN_BIAS + 1)),
+        up_bgrad[0],
     )
     own_small, own_qkv_grad, own_output, own_up, own_down = scatter_all(
         (small_grads, qkv_wgrad, output_wgrad, up_wgrad, down_wgrad), scatter_chunks(), 1
     )
     return (
-        block_out,
+        block_out.reshape(activations.shape),
         input_grad,
         own_qkv_grad[:, :width],
         own_qkv_grad[:, width : 2 * width],

time: 584 us -> 507 us (0.87)
  matrix products: 125 us -> 17.4 us
  Pallas kernels: 367 us -> 399 us
    dot_general x10 -> x0, matrix products: 106 us -> none  [the longest x1 21.5 us: fast_device(): jnp.einsum('rd,fd->rf', cot_rows, all_down, preferred_element_type=f32)]
    pallas_call x2 -> x1, Pallas kernels: 170 us -> 195 us  [forward(): pl.pallas_call(functools.partial(forward_kernel, depth, chunks, ahead), o...]
    pallas_call x1, Pallas kernels: 144 us -> 151 us  [scatter_all(): pl.pallas_call(functools.partial(rs_kernel, depth, n, chunks, lag), out_s...]
    ppermute x3 -> x2, waiting for transfers between devices: 43.4 us -> 41.5 us  [swap(): return lax.ppermute(value, 'ctx', [(0, 1), (1, 0)])]
  transfers between devices with their start and end apart: 3 -> 2, of which waited for: 3 -> 2; matrix products, arithmetic and copies ran while one was open for 6% -> 2% of each run, Pallas kernels for 0% -> 0%
where the time goes in v3:
time: 507 us; the launch traced here: 498 us
  Pallas kernels  399 us (79%)
  waiting for transfers between devices  41.5 us (8%)
  local copies, waits for them, and re-layouts  18.7 us (4%)
  other arithmetic  18 us (4%)
  matrix products  17.4 us (3%)
    pallas_call x1, Pallas kernels, forward(): pl.pallas_call(functools.partial(forward_kernel, depth, chunks, ahead), o...  195 us
    pallas_call x1, Pallas kernels, scatter_all(): pl.pallas_call(functools.partial(rs_kernel, depth, n, chunks, lag), out_s...  151 us
    pallas_call x1, Pallas kernels, attend_back(): pl.pallas_call(functools.partial(attend_back_kernel, block_rows), out_sha...  52.6 us
    ppermute x2, waiting for transfers between devices, swap(): return lax.ppermute(value, 'ctx', [(0, 1), (1, 0)])  41.5 us
    dot_general x1, matrix products, fast_device(): jnp.einsum('rd,re->de', normed_one, qkv_grad, preferred_element_type=f32)  10.3 us
  transfers between devices with their start and end apart: 2, of which 2 were waited for; matrix products, arithmetic and copies ran while one was open for 2% of the time, Pallas kernels for 0%

profile of v3, /device:TPU:0, one launch (start us, length us, event | category | flops | bytes accessed | tf_op | source)
XLA Modules:
  0.0 498.3 jit_solution(10447829314224222704)
XLA Ops:
  0.7 0.8 stack.53
  1.6 0.9 constant_dynamic-slice_fusion.2
  2.5 0.7 pad_maximum_fusion.1.refs_1_
  3.2 1.3 maximum_maximum_fusion.refs_0_
  4.5 195.5 %forward_and_feed.1 = (bf16[256,128]{1,0:T(8,128)(2,1)}, bf16[1024,1536]{1,0:T(8,128)(2,1)}, bf16[1024,1024]{1,0:T(8,128)(2,1)}, bf16[1024,4096]{1,0:T(8,128)(2,...) custom-call(bf16[16,128]{1,0:T(8,128)(2,1)} %maximum_maximum_fusion., ...), custom_call_target="tpu_custom_call" | custom-call | tf_op jit(solution)/shard_map/forward_and_feed/pallas_call | solution.py:927
  200.1 2.4 constant_dynamic-slice_fusion.1
  202.5 1.0 collective-permute-start
  203.9 0.8 slice.128
  204.8 0.6 fusion.4
  205.4 16.9 %collective-permute-done = bf16[784,512]{1,0:T(8,128)(2,1)} collective-permute-done((bf16[784,512]{1,0:T(8,128)(2,1)}, bf16[784,512]{1,0:T(8,128)(2,1)}, u32[]{:S(2)}, u32[]{:S(2)}) %collective-permute-start) | collective-permute-done | bytes 802848 | tf_op jit(solution)/shard_map/ppermute | solution.py:1074
  222.2 2.4 pad_maximum_fusion.grads
  224.6 52.6 %attend_back.1 = bf16[1568,1536]{1,0:T(8,128)(2,1)} custom-call(bf16[1568,1536]{1,0:T(8,128)(2,1)} %get-tuple-element.39.qkv, f32[1568,512]{1,0:T(8,128)} %get-tuple-element.40.attended, f32[1568,512]{1,0:T(8,128)} %get-tuple-element.41.inverse, bf16[1568,512]{1,0:T(8,128)(2,1)} %pad_maximum_fusion.grads, bf16[8,1568,1568]{2,1,0:T(8,128)(2,1)} %get-tuple-element.43.weights_in), custom_call_target="tpu_custom_call" | custom-call | tf_op jit(solution)/shard_map/attend_back/pallas_call | solution.py:1036
  277.3 3.3 convert_reduce_fusion
  280.6 0.5 copy-done.3
  281.1 7.2 %fusion.19 = f32[1568,1024]{1,0:T(8,128)S(1)} fusion(bf16[1568,1536]{1,0:T(8,128)(2,1)S(1)} %copy-done.3, bf16[1024,1536]{1,0:T(8,128)(2,1)} %get-tuple-element.44), kind=kOutput, calls=%fused_computation.56 | convolution fusion | flops 4932501504 | bytes 14385152 | tf_op jit(solution)/shard_map/re,de->rd/dot_general | solution.py:1120
  288.3 2.7 copy-done.4
  291.0 1.4 slice.127
  292.4 1.0 collective-permute-start.1
  293.6 10.3 %convolution_convert_fusion.refs_1_ = bf16[1024,1536]{1,0:T(8,128)(2,1)} fusion(bf16[1568,1024]{1,0:T(8,128)(2,1)} %get-tuple-element.48, bf16[1568,1536]{1,0:T(8,128)(2,1)} %attend_back.1), kind=kOutput, calls=%fused_computation.8 | convolution fusion | flops 4934074368 | bytes 11173888 | tf_op jit(solution)/shard_map/rd,re->de/dot_general | solution.py:1115
  303.9 24.6 %collective-permute-done.1 = bf16[784,1024]{1,0:T(8,128)(2,1)} collective-permute-done((bf16[784,1024]{1,0:T(8,128)(2,1)}, bf16[784,1024]{1,0:T(8,128)(2,1)}, u32[]{:S(2)}, u32[]{:S(2)}) %collective-permute-start.1) | collective-permute-done | bytes 1605664 | tf_op jit(solution)/shard_map/ppermute | solution.py:1074
  328.5 2.8 fusion.7
  331.5 0.7 fusion.10
  332.2 151.4 %gradients_scatter.1 = (f32[16,128]{1,0:T(8,128)}, f32[64,3072]{1,0:T(8,128)}, f32[64,1024]{1,0:T(8,128)}, f32[64,4096]{1,0:T(8,128)}, f32[256,1024]{1,0:T(8,128)}) custom-call(bf16[256,128]{1,0:T(8,128)(2,1)} %bitcast.55, bf16[1024,1536]{1,0:T(8,128)(2,1)} %convolution_convert_fusion.refs_1_, bf16[1024,1024]{1,0:T(8,128)(2,1)} %get-tuple-element.49.refs_2_, ...), custom_call_target="tpu_custom_call" | custom-call | tf_op jit(solution)/shard_map/gradients_scatter/pallas_call | solution.py:567
  483.6 1.5 slice_bitcast_fusion.1
  485.1 1.2 slice_bitcast_fusion
  486.3 2.0 fusion.17
  488.4 3.8 fusion.16
  492.2 2.1 add_bitcast_fusion
  494.3 1.2 copy.44
  495.4 0.7 copy.45
  496.1 1.0 copy.46
  497.1 1.0 copy.47
  (49 shorter events, 1.1 us)
Async XLA Ops:
  0.7 1.0 copy-start
  4.5 199.0 %copy-start.2 = (bf16[1,784,1024]{2,1,0:T(8,128)(2,1)S(1)}, bf16[1,784,1024]{2,1,0:T(8,128)(2,1)}, u32[]{:S(2)}) copy-start(bf16[1,784,1024]{2,1,0:T(8,128)(2,1)} %param.17) | copy-start | bytes 4816900
  200.0 3.5 copy-start.11
  200.0 4.7 copy-start.12
  202.5 19.8 %collective-permute-start = (bf16[784,512]{1,0:T(8,128)(2,1)}, bf16[784,512]{1,0:T(8,128)(2,1)}, u32[]{:S(2)}, u32[]{:S(2)}) collective-permute-start(bf16[784,512]{1,0:T(8,128)(2,1)} %get-tuple-element.63), channel_id=1, source_target_pairs={{0,1},{1,0},{2,3},{3,2},{4,5},{5,4},{6,7},{7,6},{8,9},{9,8},{10,11... | collective-permute-start | bytes 2408456 | tf_op jit(solution)/shard_map/ppermute | solution.py:1074
  277.3 3.8 copy-start.3
  288.3 2.7 copy-start.4
  291.0 2.4 copy-start.13
  292.4 36.1 %collective-permute-start.1 = (bf16[784,1024]{1,0:T(8,128)(2,1)}, bf16[784,1024]{1,0:T(8,128)(2,1)}, u32[]{:S(2)}, u32[]{:S(2)}) collective-permute-start(bf16[784,1024]{1,0:T(8,128)(2,1)} %slice.127), channel_id=1, source_target_pairs={{0,1},{1,0},{2,3},{3,2},{4,5},{5,4},{6,7},{7,6},{8,9},{9,8},{10,11... | collective-permute-start | bytes 4816904 | tf_op jit(solution)/shard_map/ppermute | solution.py:1074
  293.6 34.9 %copy-start.5 = (f32[1568,1024]{1,0:T(8,128)S(1)}, f32[1568,1024]{1,0:T(8,128)}, u32[]{:S(2)}) copy-start(f32[1568,1024]{1,0:T(8,128)} %copy-done.4) | copy-start | bytes 19267588
  488.4 3.8 copy-start.6
  492.2 2.1 copy-start.7
  494.2 1.2 copy-start.10
  494.2 1.9 copy-start.9
  494.2 2.9 copy-start.8
  494.2 3.8 copy-start.1
